TPU v7x, 256 devices: a whole 4x4x8 slice. The times are simulated.
256 devices in a mesh: gx: 16 (over y, z_lo, core), gy: 16 (over x, z_hi).
Axes of the slice: x: 4, y: 4, z: 8 (z_hi: 4, z_lo: 2; z = z_hi * 2 + z_lo), core: 2. Of those that a mesh axis runs over, the one named last changes fastest.
Arguments:
- load: float32 [3, 256, 256, 128], P(None, 'gx', 'gy'), may hold values from -24 to 24
- guess: float32 [3, 256, 256, 128], P(None, 'gx', 'gy'), may hold values from -1.2 to 1.2
- labels: int32 [256, 256, 128], P('gx', 'gy'), may hold values from 0 to 2
- segments: int32 [256, 256, 128], P('gx', 'gy'), may hold values from 0 to 15
- stiffness: float32 [6, 48], replicated, as said below
Outputs:
- displacement: float32 [3, 256, 256, 128], P(None, 'gx', 'gy')
- residual: float32 [3, 256, 256, 128], P(None, 'gx', 'gy')
Inputs may be any that keep to these rules, and one draw needn't show every extreme that they name: `stiffness`: for each of the 48 entries the six values form a symmetric positive definite 3x3 matrix.
All inputs are finite; a program needn't handle non-finite values.
Results may differ from a plain program's by a relative error of at most 0.00018.
Values sent between devices are 32-bit elements; how exact they have to be, the bound alone decides.
A program may use at most 64 MiB of HBM per device.

v0:
```python
import jax
import jax.numpy as jnp
from jax import lax
from jax.sharding import PartitionSpec as P

SEGS = 16


theta_value = 1.025
delta_value = 0.975
vector_signs = (-1.0, -1.0, 1.0)
tensor_signs = (1.0, 1.0, 1.0, 1.0, -1.0, -1.0)


def padded_2(cells, sides, width, closed):
    for axis, dim in sides:
        count = lax.axis_size(axis)
        ends = count if closed else count - 1
        head = lax.slice_in_dim(cells, 0, width, axis=dim)
        tail = lax.slice_in_dim(cells, cells.shape[dim] - width, cells.shape[dim], axis=dim)
        cells = jnp.concatenate(
            [
                lax.ppermute(tail, axis, [(i, (i + 1) % count) for i in range(ends)]),
                cells,
                lax.ppermute(head, axis, [((i + 1) % count, i) for i in range(ends)]),
            ],
            axis=dim,
        )
    return cells


def partner_2(array, axis, apart):
    return lax.ppermute(array, axis, [(i, i ^ 1 << apart) for i in range(lax.axis_size(axis))])


def extend(field, signs):
    cells_x = field.shape[1]
    widened = padded_2(field, (("gy", 2),), 1, True)
    extended = padded_2(widened, (("gx", 1),), 1, False)
    end_planes = jnp.stack([widened[:, 0], widened[:, cells_x - 1]], axis=0)
    bit_count = lax.axis_size("gy").bit_length() - 1
    bit_order = list(range(bit_count))
    partner = end_planes
    for bit_index in bit_order:
        partner = partner_2(partner, "gy", bit_index)
    scaling = jnp.asarray(signs, jnp.float32).reshape(1, -1, 1, 1)
    mirrored = partner[:, :, ::-1] * scaling
    column_index = lax.axis_index("gx")
    last_column = lax.axis_size("gx") - 1
    low_ghost = jnp.where(column_index == 0, mirrored[0], extended[:, 0])
    high_ghost = jnp.where(column_index == last_column, mirrored[1], extended[:, cells_x + 1])
    return jnp.concatenate(
        [low_ghost[:, None], extended[:, 1 : cells_x + 1], high_ghost[:, None]], axis=1
    )


def lookup(code_field, stiffness):
    flat_codes = code_field[0].reshape(1, -1)
    table_ids = jnp.arange(stiffness.shape[1], dtype=jnp.float32).reshape(-1, 1)
    selector = (table_ids == flat_codes).astype(jnp.float32)
    coef_flat = jnp.dot(
        stiffness, selector, precision=lax.Precision.HIGHEST, preferred_element_type=jnp.float32
    )
    return coef_flat.reshape((stiffness.shape[0],) + code_field.shape[1:])


def smooth(padded):
    along_x = padded[:, 1:-1] + 0.5 * (padded[:, :-2] + padded[:, 2:])
    along_y = along_x[:, :, 1:-1] + 0.5 * (along_x[:, :, :-2] + along_x[:, :, 2:])
    return along_y[..., 1:-1] + 0.5 * (along_y[..., :-2] + along_y[..., 2:])


def sym_apply(coef, vector):
    return jnp.stack(
        [
            coef[0] * vector[0] + coef[3] * vector[1] + coef[4] * vector[2],
            coef[3] * vector[0] + coef[1] * vector[1] + coef[5] * vector[2],
            coef[4] * vector[0] + coef[5] * vector[1] + coef[2] * vector[2],
        ]
    )


def operate(field, coef_ext, coef_sum):
    field_ext = extend(field, vector_signs)
    product_ext = sym_apply(coef_ext, field_ext)
    stacked = jnp.concatenate([field_ext, product_ext], axis=0)
    sums = smooth(jnp.pad(stacked, ((0, 0), (0, 0), (0, 0), (1, 1))))
    interior = coef_ext[:, 1:-1, 1:-1]
    product = product_ext[:, 1:-1, 1:-1]
    return 0.5 * (
        8.0 * product + sym_apply(coef_sum, field) - sym_apply(interior, sums[:3]) - sums[3:]
    )


def body(load, guess, labels, segments, stiffness):
    codes = (labels.astype(jnp.float32) * SEGS + segments.astype(jnp.float32))[None]
    coef_ext = extend(lookup(codes, stiffness), tensor_signs)
    coef_sum = smooth(jnp.pad(coef_ext, ((0, 0), (0, 0), (0, 0), (1, 1)), mode="edge"))
    interior = coef_ext[:, 1:-1, 1:-1]
    inverse = 1.0 / (0.5 * (6.0 * interior[:3] + coef_sum[:3]))
    sigma = theta_value / delta_value
    residual = load - operate(guess, coef_ext, coef_sum)
    rho_prev = 1.0 / sigma
    update = inverse * residual / theta_value
    displacement = guess + update
    residual = load - operate(displacement, coef_ext, coef_sum)
    rho_now = 1.0 / (2.0 * sigma - rho_prev)
    update = rho_now * rho_prev * update + 2.0 * rho_now / delta_value * inverse * residual
    displacement = displacement + update
    return (displacement, residual)


def solution(mesh):
    return jax.shard_map(
        body,
        mesh=mesh,
        in_specs=(
            P(None, "gx", "gy", None),
            P(None, "gx", "gy", None),
            P("gx", "gy", None),
            P("gx", "gy", None),
            P(),
        ),
        out_specs=(P(None, "gx", "gy", None), P(None, "gx", "gy", None)),
        check_vma=False,
    )
```

profile of v0, /device:TPU:49, one launch (start us, length us, event | category | flops | bytes accessed | tf_op | source)
XLA Modules:
  0.0 134.6 jit_solution(16613382912057498598)
XLA Ops:
  0.6 1.0 convert_add_fusion
  1.7 1.9 %fusion = f32[32768,6]{0,1:T(8,128)S(1)} fusion(f32[6,48]{1,0:T(8,128)S(1)} %copy-done, f32[32768]{0:T(1024)S(1)} %bitcast.113), kind=kOutput, calls=%fused_computation.1 | convolution fusion | flops 114819072 | bytes 918656 | tf_op jit(solution)/shard_map/dot_general | solution.py:61
  3.5 0.1 copy.10
  3.8 3.1 %collective-permute-start = (f32[6,16,1,128]{3,2,0,1:T(1,128)S(1)}, f32[6,16,1,128]{3,2,0,1:T(1,128)S(1)}, u32[]{:S(2)}, u32[]{:S(2)}) collective-permute-start(f32[6,16,1,128]{3,2,0,1:T(1,128)S(1)} %get-tuple-element.38), channel_id=1, source_target_pairs={{0,1},{1,2},{2,3},{3,4},{4,5},{5,6},{6,7},{7,8},{8,9},{9,10},{10,1... | collective-permute-start | bytes 147464 | tf_op jit(solution)/shard_map/ppermute | solution.py:23
  6.8 4.4 %collective-permute-start.1 = (f32[6,16,1,128]{3,2,0,1:T(1,128)S(1)}, f32[6,16,1,128]{3,2,0,1:T(1,128)S(1)}, u32[]{:S(2)}, u32[]{:S(2)}) collective-permute-start(f32[6,16,1,128]{3,2,0,1:T(1,128)S(1)} %get-tuple-element.39), channel_id=1, source_target_pairs={{1,0},{2,1},{3,2},{4,3},{5,4},{6,5},{7,6},{8,7},{9,8},{10,9},{11,1... | collective-permute-start | bytes 147464 | tf_op jit(solution)/shard_map/ppermute | solution.py:25
  11.4 5.7 %collective-permute-start.9 = (f32[3,16,1,128]{3,2,0,1:T(1,128)S(1)}, f32[3,16,1,128]{3,2,0,1:T(1,128)S(1)}, u32[]{:S(2)}, u32[]{:S(2)}) collective-permute-start(f32[3,16,1,128]{3,2,0,1:T(1,128)S(1)} %get-tuple-element.49), channel_id=1, source_target_pairs={{1,0},{2,1},{3,2},{4,3},{5,4},{6,5},{7,6},{8,7},{9,8},{10,9},{11,1... | collective-permute-start | bytes 73736 | tf_op jit(solution)/shard_map/ppermute | solution.py:25
  17.0 1.2 fusion.46
  18.4 0.7 collective-permute-start.10
  19.1 0.2 pad_maximum_fusion.3
  19.3 3.4 %collective-permute-done.10 = f32[2,3,18,128]{3,2,1,0:T(8,128)S(1)} collective-permute-done((f32[2,3,18,128]{3,2,1,0:T(8,128)S(1)}, f32[2,3,18,128]{3,2,1,0:T(8,128)S(1)}, u32[]{:S(2)}, u32[]{:S(2)}) %collective-permute-start.10) | collective-permute-done | bytes 55328 | tf_op jit(solution)/shard_map/ppermute | solution.py:33
  22.7 1.0 collective-permute-start.11
  23.7 6.1 %collective-permute-done.11 = f32[2,3,18,128]{3,2,1,0:T(8,128)S(1)} collective-permute-done((f32[2,3,18,128]{3,2,1,0:T(8,128)S(1)}, f32[2,3,18,128]{3,2,1,0:T(8,128)S(1)}, u32[]{:S(2)}, u32[]{:S(2)}) %collective-permute-start.11) | collective-permute-done | bytes 55328 | tf_op jit(solution)/shard_map/ppermute | solution.py:33
  29.9 3.1 %collective-permute-start.2 = (f32[2,6,18,128]{3,2,1,0:T(8,128)S(1)}, f32[2,6,18,128]{3,2,1,0:T(8,128)S(1)}, u32[]{:S(2)}, u32[]{:S(2)}) collective-permute-start(f32[2,6,18,128]{3,2,1,0:T(8,128)S(1)} %pad_maximum_fusion.11), channel_id=1, source_target_pairs={{0,1},{1,0},{2,3},{3,2},{4,5},{5,4},{6,7},{7,6},{8,9},{9,8},{10,11... | collective-permute-start | bytes 331784 | tf_op jit(solution)/shard_map/ppermute | solution.py:33
  32.9 0.4 collective-permute-done.12
  33.3 1.3 collective-permute-start.13
  34.8 9.9 %collective-permute-start.14 = (f32[3,1,18,128]{3,2,0,1:T(8,128)S(1)}, f32[3,1,18,128]{3,2,0,1:T(8,128)S(1)}, u32[]{:S(2)}, u32[]{:S(2)}) collective-permute-start(f32[3,1,18,128]{3,2,0,1:T(8,128)S(1)} %get-tuple-element.40), channel_id=1, source_target_pairs={{0,16},{16,32},{32,48},{48,64},{64,80},{80,96},{96,112},{112,128},... | collective-permute-start | bytes 82952 | tf_op jit(solution)/shard_map/ppermute | solution.py:23
  44.7 1.9 %collective-permute-start.15 = (f32[3,1,18,128]{3,2,1,0:T(8,128)S(1)}, f32[3,1,18,128]{3,2,1,0:T(8,128)S(1)}, u32[]{:S(2)}, u32[]{:S(2)}) collective-permute-start(f32[3,1,18,128]{3,2,1,0:T(8,128)S(1)} %get-tuple-element.43), channel_id=1, source_target_pairs={{16,0},{32,16},{48,32},{64,48},{80,64},{96,80},{112,96},{128,112},... | collective-permute-start | bytes 82952 | tf_op jit(solution)/shard_map/ppermute | solution.py:25
  46.6 4.5 %collective-permute-start.6 = (f32[6,1,18,128]{3,2,0,1:T(8,128)S(1)}, f32[6,1,18,128]{3,2,0,1:T(8,128)S(1)}, u32[]{:S(2)}, u32[]{:S(2)}) collective-permute-start(f32[6,1,18,128]{3,2,0,1:T(8,128)S(1)} %get-tuple-element.22), channel_id=1, source_target_pairs={{0,16},{16,32},{32,48},{48,64},{64,80},{80,96},{96,112},{112,128},... | collective-permute-start | bytes 165896 | tf_op jit(solution)/shard_map/ppermute | solution.py:23
  51.2 1.9 %collective-permute-start.7 = (f32[6,1,18,128]{3,2,1,0:T(8,128)S(1)}, f32[6,1,18,128]{3,2,1,0:T(8,128)S(1)}, u32[]{:S(2)}, u32[]{:S(2)}) collective-permute-start(f32[6,1,18,128]{3,2,1,0:T(8,128)S(1)} %get-tuple-element.25), channel_id=1, source_target_pairs={{16,0},{32,16},{48,32},{64,48},{80,64},{96,80},{112,96},{128,112},... | collective-permute-start | bytes 165896 | tf_op jit(solution)/shard_map/ppermute | solution.py:25
  53.1 4.8 %collective-permute-start.3 = (f32[2,6,18,128]{3,2,1,0:T(8,128)S(1)}, f32[2,6,18,128]{3,2,1,0:T(8,128)S(1)}, u32[]{:S(2)}, u32[]{:S(2)}) collective-permute-start(f32[2,6,18,128]{3,2,1,0:T(8,128)S(1)} %collective-permute-done.2), channel_id=1, source_target_pairs={{0,2},{1,3},{2,0},{3,1},{4,6},{5,7},{6,4},{7,5},{8,10},{9,11},{10,... | collective-permute-start | bytes 331784 | tf_op jit(solution)/shard_map/ppermute | solution.py:33
  58.1 7.5 %collective-permute-done.3 = f32[2,6,18,128]{3,2,1,0:T(8,128)S(1)} collective-permute-done((f32[2,6,18,128]{3,2,1,0:T(8,128)S(1)}, f32[2,6,18,128]{3,2,1,0:T(8,128)S(1)}, u32[]{:S(2)}, u32[]{:S(2)}) %collective-permute-start.3) | collective-permute-done | bytes 110624 | tf_op jit(solution)/shard_map/ppermute | solution.py:33
  65.7 4.6 %collective-permute-done.4 = f32[2,6,18,128]{3,2,1,0:T(8,128)S(1)} collective-permute-done((f32[2,6,18,128]{3,2,1,0:T(8,128)S(1)}, f32[2,6,18,128]{3,2,1,0:T(8,128)S(1)}, u32[]{:S(2)}, u32[]{:S(2)}) %collective-permute-start.4) | collective-permute-done | bytes 110624 | tf_op jit(solution)/shard_map/ppermute | solution.py:33
  70.3 1.5 %collective-permute-start.5 = (f32[2,6,18,128]{3,2,1,0:T(8,128)S(1)}, f32[2,6,18,128]{3,2,1,0:T(8,128)S(1)}, u32[]{:S(2)}, u32[]{:S(2)}) collective-permute-start(f32[2,6,18,128]{3,2,1,0:T(8,128)S(1)} %collective-permute-done.4), channel_id=1, source_target_pairs={{0,8},{1,9},{2,10},{3,11},{4,12},{5,13},{6,14},{7,15},{8,0},{9,1},... | collective-permute-start | bytes 331784 | tf_op jit(solution)/shard_map/ppermute | solution.py:33
  71.8 1.0 pad_maximum_fusion.4
  72.8 3.0 %collective-permute-done.5 = f32[2,6,18,128]{3,2,1,0:T(8,128)S(1)} collective-permute-done((f32[2,6,18,128]{3,2,1,0:T(8,128)S(1)}, f32[2,6,18,128]{3,2,1,0:T(8,128)S(1)}, u32[]{:S(2)}, u32[]{:S(2)}) %collective-permute-start.5) | collective-permute-done | bytes 110624 | tf_op jit(solution)/shard_map/ppermute | solution.py:33
  76.0 0.2 pad_maximum_fusion.1
  76.2 0.4 fusion.44
  76.6 1.1 pad_maximum_fusion
  77.8 0.2 fusion.7
  78.0 0.4 fusion.13
  78.4 0.7 copy-done.2
  79.2 0.6 copy-done.20
  79.9 0.8 select_maximum_fusion
  80.7 0.2 fusion.5
  80.9 0.4 fusion.11
  81.3 0.9 fusion.17
  82.4 0.8 copy-done.12
  83.4 1.0 multiply_add_fusion
  84.4 1.6 %collective-permute-start.16 = (f32[3,16,1,128]{3,2,0,1:T(1,128)S(1)}, f32[3,16,1,128]{3,2,0,1:T(1,128)S(1)}, u32[]{:S(2)}, u32[]{:S(2)}) collective-permute-start(f32[3,16,1,128]{3,2,0,1:T(1,128)S(1)} %get-tuple-element.46), channel_id=1, source_target_pairs={{0,1},{1,2},{2,3},{3,4},{4,5},{5,6},{6,7},{7,8},{8,9},{9,10},{10,1... | collective-permute-start | bytes 73736 | tf_op jit(solution)/shard_map/ppermute | solution.py:23
  85.9 4.2 %collective-permute-start.17 = (f32[3,16,1,128]{3,2,0,1:T(1,128)S(1)}, f32[3,16,1,128]{3,2,0,1:T(1,128)S(1)}, u32[]{:S(2)}, u32[]{:S(2)}) collective-permute-start(f32[3,16,1,128]{3,2,0,1:T(1,128)S(1)} %get-tuple-element.47), channel_id=1, source_target_pairs={{1,0},{2,1},{3,2},{4,3},{5,4},{6,5},{7,6},{8,7},{9,8},{10,9},{11,1... | collective-permute-start | bytes 73736 | tf_op jit(solution)/shard_map/ppermute | solution.py:25
  90.1 1.2 collective-permute-done.16
  91.3 0.6 pad_maximum_fusion.14
  92.0 0.8 pad_maximum_fusion.13
  92.8 2.8 %collective-permute-start.18 = (f32[2,3,18,128]{3,2,1,0:T(8,128)S(1)}, f32[2,3,18,128]{3,2,1,0:T(8,128)S(1)}, u32[]{:S(2)}, u32[]{:S(2)}) collective-permute-start(f32[2,3,18,128]{3,2,1,0:T(8,128)S(1)} %pad_maximum_fusion.13), channel_id=1, source_target_pairs={{0,1},{1,0},{2,3},{3,2},{4,5},{5,4},{6,7},{7,6},{8,9},{9,8},{10,11... | collective-permute-start | bytes 165896 | tf_op jit(solution)/shard_map/ppermute | solution.py:33
  95.6 1.7 %collective-permute-done.18 = f32[2,3,18,128]{3,2,1,0:T(8,128)S(1)} collective-permute-done((f32[2,3,18,128]{3,2,1,0:T(8,128)S(1)}, f32[2,3,18,128]{3,2,1,0:T(8,128)S(1)}, u32[]{:S(2)}, u32[]{:S(2)}) %collective-permute-start.18) | collective-permute-done | bytes 55328 | tf_op jit(solution)/shard_map/ppermute | solution.py:33
  97.3 2.5 %collective-permute-start.19 = (f32[2,3,18,128]{3,2,1,0:T(8,128)S(1)}, f32[2,3,18,128]{3,2,1,0:T(8,128)S(1)}, u32[]{:S(2)}, u32[]{:S(2)}) collective-permute-start(f32[2,3,18,128]{3,2,1,0:T(8,128)S(1)} %collective-permute-done.18), channel_id=1, source_target_pairs={{0,2},{1,3},{2,0},{3,1},{4,6},{5,7},{6,4},{7,5},{8,10},{9,11},{10,... | collective-permute-start | bytes 165896 | tf_op jit(solution)/shard_map/ppermute | solution.py:33
  99.9 4.7 %collective-permute-done.19 = f32[2,3,18,128]{3,2,1,0:T(8,128)S(1)} collective-permute-done((f32[2,3,18,128]{3,2,1,0:T(8,128)S(1)}, f32[2,3,18,128]{3,2,1,0:T(8,128)S(1)}, u32[]{:S(2)}, u32[]{:S(2)}) %collective-permute-start.19) | collective-permute-done | bytes 55328 | tf_op jit(solution)/shard_map/ppermute | solution.py:33
  104.6 0.8 collective-permute-start.20
  105.4 2.4 %collective-permute-done.20 = f32[2,3,18,128]{3,2,1,0:T(8,128)S(1)} collective-permute-done((f32[2,3,18,128]{3,2,1,0:T(8,128)S(1)}, f32[2,3,18,128]{3,2,1,0:T(8,128)S(1)}, u32[]{:S(2)}, u32[]{:S(2)}) %collective-permute-start.20) | collective-permute-done | bytes 55328 | tf_op jit(solution)/shard_map/ppermute | solution.py:33
  107.8 0.6 collective-permute-start.21
  108.3 0.8 multiply_add_fusion.12
  109.1 11.7 %collective-permute-start.22 = (f32[3,1,18,128]{3,2,0,1:T(8,128)}, f32[3,1,18,128]{3,2,0,1:T(8,128)}, u32[]{:S(2)}, u32[]{:S(2)}) collective-permute-start(f32[3,1,18,128]{3,2,0,1:T(8,128)} %get-tuple-element.44), channel_id=1, source_target_pairs={{0,16},{16,32},{32,48},{48,64},{64,80},{80,96},{96,112},{112,128},... | collective-permute-start | bytes 82952 | tf_op jit(solution)/shard_map/ppermute | solution.py:23
  120.9 2.1 %collective-permute-start.23 = (f32[3,1,18,128]{3,2,0,1:T(8,128)}, f32[3,1,18,128]{3,2,0,1:T(8,128)}, u32[]{:S(2)}, u32[]{:S(2)}) collective-permute-start(f32[3,1,18,128]{3,2,0,1:T(8,128)} %get-tuple-element.45), channel_id=1, source_target_pairs={{16,0},{32,16},{48,32},{64,48},{80,64},{96,80},{112,96},{128,112},... | collective-permute-start | bytes 82952 | tf_op jit(solution)/shard_map/ppermute | solution.py:25
  123.0 0.9 rev.11
  124.0 3.3 %collective-permute-done.23 = f32[3,1,18,128]{3,2,0,1:T(8,128)} collective-permute-done((f32[3,1,18,128]{3,2,0,1:T(8,128)}, f32[3,1,18,128]{3,2,0,1:T(8,128)}, u32[]{:S(2)}, u32[]{:S(2)}) %collective-permute-start.23) | collective-permute-done | bytes 27680 | tf_op jit(solution)/shard_map/ppermute | solution.py:25
  127.4 0.8 fusion.38
  128.4 0.1 pad_maximum_fusion.2
  128.5 1.9 %fusion.3 = (f32[6,16,18,130]{3,2,0,1:T(8,128)S(1)}, f32[6,16,18,130]{3,2,0,1:T(8,128)S(1)}) fusion(f32[6,18,18,128]{3,2,0,1:T(8,128)S(1)} %pad_maximum_fusion.2), kind=kLoop, calls=%fused_computation.15 | loop fusion | flops 224640 | bytes 2792448 | tf_op jit(solution)/shard_map/add | solution.py:68
  130.4 0.3 copy_add_fusion
  130.7 0.4 fusion.9
  131.2 0.5 fusion.15
  131.6 0.4 copy-done.7
  132.4 0.9 copy-done.4
  133.5 1.1 add_add_fusion
  (92 shorter events, 2.3 us)
Async XLA Ops:
  0.6 1.0 copy-start
  1.7 9.6 %copy-start.1 = (f32[3,16,16,128]{3,2,1,0:T(8,128)S(1)}, f32[3,16,16,128]{3,2,1,0:T(8,128)}, u32[]{:S(2)}) copy-start(f32[3,16,16,128]{3,2,1,0:T(8,128)} %param.9) | copy-start | bytes 1179652
  3.8 15.3 %collective-permute-start = (f32[6,16,1,128]{3,2,0,1:T(1,128)S(1)}, f32[6,16,1,128]{3,2,0,1:T(1,128)S(1)}, u32[]{:S(2)}, u32[]{:S(2)}) collective-permute-start(f32[6,16,1,128]{3,2,0,1:T(1,128)S(1)} %get-tuple-element.38), channel_id=1, source_target_pairs={{0,1},{1,2},{2,3},{3,4},{4,5},{5,6},{6,7},{7,8},{8,9},{9,10},{10,1... | collective-permute-start | bytes 147464 | tf_op jit(solution)/shard_map/ppermute | solution.py:23
  6.8 12.3 %collective-permute-start.1 = (f32[6,16,1,128]{3,2,0,1:T(1,128)S(1)}, f32[6,16,1,128]{3,2,0,1:T(1,128)S(1)}, u32[]{:S(2)}, u32[]{:S(2)}) collective-permute-start(f32[6,16,1,128]{3,2,0,1:T(1,128)S(1)} %get-tuple-element.39), channel_id=1, source_target_pairs={{1,0},{2,1},{3,2},{4,3},{5,4},{6,5},{7,6},{8,7},{9,8},{10,9},{11,1... | collective-permute-start | bytes 147464 | tf_op jit(solution)/shard_map/ppermute | solution.py:25
  11.3 7.0 %collective-permute-start.8 = (f32[3,16,1,128]{3,2,0,1:T(1,128)S(1)}, f32[3,16,1,128]{3,2,0,1:T(1,128)S(1)}, u32[]{:S(2)}, u32[]{:S(2)}) collective-permute-start(f32[3,16,1,128]{3,2,0,1:T(1,128)S(1)} %get-tuple-element.48), channel_id=1, source_target_pairs={{0,1},{1,2},{2,3},{3,4},{4,5},{5,6},{6,7},{7,8},{8,9},{9,10},{10,1... | collective-permute-start | bytes 73736 | tf_op jit(solution)/shard_map/ppermute | solution.py:23
  11.4 6.9 %collective-permute-start.9 = (f32[3,16,1,128]{3,2,0,1:T(1,128)S(1)}, f32[3,16,1,128]{3,2,0,1:T(1,128)S(1)}, u32[]{:S(2)}, u32[]{:S(2)}) collective-permute-start(f32[3,16,1,128]{3,2,0,1:T(1,128)S(1)} %get-tuple-element.49), channel_id=1, source_target_pairs={{1,0},{2,1},{3,2},{4,3},{5,4},{6,5},{7,6},{8,7},{9,8},{10,9},{11,1... | collective-permute-start | bytes 73736 | tf_op jit(solution)/shard_map/ppermute | solution.py:25
  18.3 64.1 %copy-start.6 = (f32[1,32768]{1,0:T(1,128)}, f32[1,32768]{1,0:T(1,128)S(1)}, u32[]{:S(2)}) copy-start(f32[1,32768]{1,0:T(1,128)S(1)} %get-tuple-element.27) | copy-start | bytes 393220
  18.3 64.1 %copy-start.8 = (f32[1,32768]{1,0:T(1,128)}, f32[1,32768]{1,0:T(1,128)S(1)}, u32[]{:S(2)}) copy-start(f32[1,32768]{1,0:T(1,128)S(1)} %get-tuple-element.28) | copy-start | bytes 393220
  18.3 64.1 %copy-start.10 = (f32[1,32768]{1,0:T(1,128)}, f32[1,32768]{1,0:T(1,128)S(1)}, u32[]{:S(2)}) copy-start(f32[1,32768]{1,0:T(1,128)S(1)} %get-tuple-element.29) | copy-start | bytes 393220
  18.3 53.5 %copy-start.19 = (f32[3,16,1,128]{3,2,0,1:T(1,128)}, f32[3,16,1,128]{3,2,0,1:T(1,128)S(1)}, u32[]{:S(2)}) copy-start(f32[3,16,1,128]{3,2,0,1:T(1,128)S(1)} %collective-permute-done.9) | copy-start | bytes 73732
  18.4 4.3 %collective-permute-start.10 = (f32[2,3,18,128]{3,2,1,0:T(8,128)S(1)}, f32[2,3,18,128]{3,2,1,0:T(8,128)S(1)}, u32[]{:S(2)}, u32[]{:S(2)}) collective-permute-start(f32[2,3,18,128]{3,2,1,0:T(8,128)S(1)} %pad_maximum_fusion.12), channel_id=1, source_target_pairs={{0,1},{1,0},{2,3},{3,2},{4,5},{5,4},{6,7},{7,6},{8,9},{9,8},{10,11... | collective-permute-start | bytes 165896 | tf_op jit(solution)/shard_map/ppermute | solution.py:33
  19.3 38.7 %copy-start.25 = (f32[3]{0:T(128)S(1)}, f32[3]{0:T(128)}, u32[]{:S(2)}) copy-start(f32[3]{0:T(128)} %constant.37.clone) | copy-start | bytes 40
  22.7 7.1 %collective-permute-start.11 = (f32[2,3,18,128]{3,2,1,0:T(8,128)S(1)}, f32[2,3,18,128]{3,2,1,0:T(8,128)S(1)}, u32[]{:S(2)}, u32[]{:S(2)}) collective-permute-start(f32[2,3,18,128]{3,2,1,0:T(8,128)S(1)} %collective-permute-done.10), channel_id=1, source_target_pairs={{0,2},{1,3},{2,0},{3,1},{4,6},{5,7},{6,4},{7,5},{8,10},{9,11},{10,... | collective-permute-start | bytes 165896 | tf_op jit(solution)/shard_map/ppermute | solution.py:33
  29.8 3.5 %collective-permute-start.12 = (f32[2,3,18,128]{3,2,1,0:T(8,128)S(1)}, f32[2,3,18,128]{3,2,1,0:T(8,128)}, u32[]{:S(2)}, u32[]{:S(2)}) collective-permute-start(f32[2,3,18,128]{3,2,1,0:T(8,128)S(1)} %collective-permute-done.11), channel_id=1, source_target_pairs={{0,4},{1,5},{2,6},{3,7},{4,0},{5,1},{6,2},{7,3},{8,12},{9,13},{10,... | collective-permute-start | bytes 165896 | tf_op jit(solution)/shard_map/ppermute | solution.py:33
  29.9 21.3 %collective-permute-start.2 = (f32[2,6,18,128]{3,2,1,0:T(8,128)S(1)}, f32[2,6,18,128]{3,2,1,0:T(8,128)S(1)}, u32[]{:S(2)}, u32[]{:S(2)}) collective-permute-start(f32[2,6,18,128]{3,2,1,0:T(8,128)S(1)} %pad_maximum_fusion.11), channel_id=1, source_target_pairs={{0,1},{1,0},{2,3},{3,2},{4,5},{5,4},{6,7},{7,6},{8,9},{9,8},{10,11... | collective-permute-start | bytes 331784 | tf_op jit(solution)/shard_map/ppermute | solution.py:33
  33.3 19.8 %collective-permute-start.13 = (f32[2,3,18,128]{3,2,1,0:T(8,128)}, f32[2,3,18,128]{3,2,1,0:T(8,128)S(1)}, u32[]{:S(2)}, u32[]{:S(2)}) collective-permute-start(f32[2,3,18,128]{3,2,1,0:T(8,128)} %collective-permute-done.12), channel_id=1, source_target_pairs={{0,8},{1,9},{2,10},{3,11},{4,12},{5,13},{6,14},{7,15},{8,0},{9,1},... | collective-permute-start | bytes 165896 | tf_op jit(solution)/shard_map/ppermute | solution.py:33
  34.8 41.1 %copy-start.26 = (f32[6]{0:T(128)S(1)}, f32[6]{0:T(128)}, u32[]{:S(2)}) copy-start(f32[6]{0:T(128)} %constant.36.clone) | copy-start | bytes 76
  34.8 23.3 %collective-permute-start.14 = (f32[3,1,18,128]{3,2,0,1:T(8,128)S(1)}, f32[3,1,18,128]{3,2,0,1:T(8,128)S(1)}, u32[]{:S(2)}, u32[]{:S(2)}) collective-permute-start(f32[3,1,18,128]{3,2,0,1:T(8,128)S(1)} %get-tuple-element.40), channel_id=1, source_target_pairs={{0,16},{16,32},{32,48},{48,64},{64,80},{80,96},{96,112},{112,128},... | collective-permute-start | bytes 82952 | tf_op jit(solution)/shard_map/ppermute | solution.py:23
  44.7 20.9 %collective-permute-start.15 = (f32[3,1,18,128]{3,2,1,0:T(8,128)S(1)}, f32[3,1,18,128]{3,2,1,0:T(8,128)S(1)}, u32[]{:S(2)}, u32[]{:S(2)}) collective-permute-start(f32[3,1,18,128]{3,2,1,0:T(8,128)S(1)} %get-tuple-element.43), channel_id=1, source_target_pairs={{16,0},{32,16},{48,32},{64,48},{80,64},{96,80},{112,96},{128,112},... | collective-permute-start | bytes 82952 | tf_op jit(solution)/shard_map/ppermute | solution.py:25
  46.6 29.3 %collective-permute-start.6 = (f32[6,1,18,128]{3,2,0,1:T(8,128)S(1)}, f32[6,1,18,128]{3,2,0,1:T(8,128)S(1)}, u32[]{:S(2)}, u32[]{:S(2)}) collective-permute-start(f32[6,1,18,128]{3,2,0,1:T(8,128)S(1)} %get-tuple-element.22), channel_id=1, source_target_pairs={{0,16},{16,32},{32,48},{48,64},{64,80},{80,96},{96,112},{112,128},... | collective-permute-start | bytes 165896 | tf_op jit(solution)/shard_map/ppermute | solution.py:23
  51.2 24.8 %collective-permute-start.7 = (f32[6,1,18,128]{3,2,1,0:T(8,128)S(1)}, f32[6,1,18,128]{3,2,1,0:T(8,128)S(1)}, u32[]{:S(2)}, u32[]{:S(2)}) collective-permute-start(f32[6,1,18,128]{3,2,1,0:T(8,128)S(1)} %get-tuple-element.25), channel_id=1, source_target_pairs={{16,0},{32,16},{48,32},{64,48},{80,64},{96,80},{112,96},{128,112},... | collective-permute-start | bytes 165896 | tf_op jit(solution)/shard_map/ppermute | solution.py:25
  53.1 12.5 %collective-permute-start.3 = (f32[2,6,18,128]{3,2,1,0:T(8,128)S(1)}, f32[2,6,18,128]{3,2,1,0:T(8,128)S(1)}, u32[]{:S(2)}, u32[]{:S(2)}) collective-permute-start(f32[2,6,18,128]{3,2,1,0:T(8,128)S(1)} %collective-permute-done.2), channel_id=1, source_target_pairs={{0,2},{1,3},{2,0},{3,1},{4,6},{5,7},{6,4},{7,5},{8,10},{9,11},{10,... | collective-permute-start | bytes 331784 | tf_op jit(solution)/shard_map/ppermute | solution.py:33
  58.1 17.7 %copy-start.21 = (f32[3,1,18,128]{3,2,1,0:T(8,128)}, f32[3,1,18,128]{3,2,1,0:T(8,128)S(1)}, u32[]{:S(2)}) copy-start(f32[3,1,18,128]{3,2,1,0:T(8,128)S(1)} %fusion.41) | copy-start | bytes 82948
  65.6 4.7 %collective-permute-start.4 = (f32[2,6,18,128]{3,2,1,0:T(8,128)S(1)}, f32[2,6,18,128]{3,2,1,0:T(8,128)S(1)}, u32[]{:S(2)}, u32[]{:S(2)}) collective-permute-start(f32[2,6,18,128]{3,2,1,0:T(8,128)S(1)} %collective-permute-done.3), channel_id=1, source_target_pairs={{0,4},{1,5},{2,6},{3,7},{4,0},{5,1},{6,2},{7,3},{8,12},{9,13},{10,... | collective-permute-start | bytes 331784 | tf_op jit(solution)/shard_map/ppermute | solution.py:33
  65.6 10.1 %copy-start.23 = (f32[3,1,18,128]{3,2,1,0:T(8,128)}, f32[3,1,18,128]{3,2,1,0:T(8,128)S(1)}, u32[]{:S(2)}) copy-start(f32[3,1,18,128]{3,2,1,0:T(8,128)S(1)} %fusion.39) | copy-start | bytes 82948
  70.3 5.5 %collective-permute-start.5 = (f32[2,6,18,128]{3,2,1,0:T(8,128)S(1)}, f32[2,6,18,128]{3,2,1,0:T(8,128)S(1)}, u32[]{:S(2)}, u32[]{:S(2)}) collective-permute-start(f32[2,6,18,128]{3,2,1,0:T(8,128)S(1)} %collective-permute-done.4), channel_id=1, source_target_pairs={{0,8},{1,9},{2,10},{3,11},{4,12},{5,13},{6,14},{7,15},{8,0},{9,1},... | collective-permute-start | bytes 331784 | tf_op jit(solution)/shard_map/ppermute | solution.py:33
  78.0 1.1 copy-start.2
  79.1 0.7 copy-start.20
  79.1 0.8 copy-start.22
  79.1 0.8 copy-start.24
  82.2 0.9 copy-start.12
  82.2 1.0 copy-start.14
  82.2 1.1 copy-start.3
  84.4 7.0 %collective-permute-start.16 = (f32[3,16,1,128]{3,2,0,1:T(1,128)S(1)}, f32[3,16,1,128]{3,2,0,1:T(1,128)S(1)}, u32[]{:S(2)}, u32[]{:S(2)}) collective-permute-start(f32[3,16,1,128]{3,2,0,1:T(1,128)S(1)} %get-tuple-element.46), channel_id=1, source_target_pairs={{0,1},{1,2},{2,3},{3,4},{4,5},{5,6},{6,7},{7,8},{8,9},{9,10},{10,1... | collective-permute-start | bytes 73736 | tf_op jit(solution)/shard_map/ppermute | solution.py:23
  85.9 5.4 %collective-permute-start.17 = (f32[3,16,1,128]{3,2,0,1:T(1,128)S(1)}, f32[3,16,1,128]{3,2,0,1:T(1,128)S(1)}, u32[]{:S(2)}, u32[]{:S(2)}) collective-permute-start(f32[3,16,1,128]{3,2,0,1:T(1,128)S(1)} %get-tuple-element.47), channel_id=1, source_target_pairs={{1,0},{2,1},{3,2},{4,3},{5,4},{6,5},{7,6},{8,7},{9,8},{10,9},{11,1... | collective-permute-start | bytes 73736 | tf_op jit(solution)/shard_map/ppermute | solution.py:25
  92.8 4.6 %collective-permute-start.18 = (f32[2,3,18,128]{3,2,1,0:T(8,128)S(1)}, f32[2,3,18,128]{3,2,1,0:T(8,128)S(1)}, u32[]{:S(2)}, u32[]{:S(2)}) collective-permute-start(f32[2,3,18,128]{3,2,1,0:T(8,128)S(1)} %pad_maximum_fusion.13), channel_id=1, source_target_pairs={{0,1},{1,0},{2,3},{3,2},{4,5},{5,4},{6,7},{7,6},{8,9},{9,8},{10,11... | collective-permute-start | bytes 165896 | tf_op jit(solution)/shard_map/ppermute | solution.py:33
  97.3 7.2 %collective-permute-start.19 = (f32[2,3,18,128]{3,2,1,0:T(8,128)S(1)}, f32[2,3,18,128]{3,2,1,0:T(8,128)S(1)}, u32[]{:S(2)}, u32[]{:S(2)}) collective-permute-start(f32[2,3,18,128]{3,2,1,0:T(8,128)S(1)} %collective-permute-done.18), channel_id=1, source_target_pairs={{0,2},{1,3},{2,0},{3,1},{4,6},{5,7},{6,4},{7,5},{8,10},{9,11},{10,... | collective-permute-start | bytes 165896 | tf_op jit(solution)/shard_map/ppermute | solution.py:33
  104.6 3.2 %collective-permute-start.20 = (f32[2,3,18,128]{3,2,1,0:T(8,128)S(1)}, f32[2,3,18,128]{3,2,1,0:T(8,128)S(1)}, u32[]{:S(2)}, u32[]{:S(2)}) collective-permute-start(f32[2,3,18,128]{3,2,1,0:T(8,128)S(1)} %collective-permute-done.19), channel_id=1, source_target_pairs={{0,4},{1,5},{2,6},{3,7},{4,0},{5,1},{6,2},{7,3},{8,12},{9,13},{10,... | collective-permute-start | bytes 165896 | tf_op jit(solution)/shard_map/ppermute | solution.py:33
  107.8 15.3 %collective-permute-start.21 = (f32[2,3,18,128]{3,2,1,0:T(8,128)S(1)}, f32[2,3,18,128]{3,2,1,0:T(8,128)}, u32[]{:S(2)}, u32[]{:S(2)}) collective-permute-start(f32[2,3,18,128]{3,2,1,0:T(8,128)S(1)} %collective-permute-done.20), channel_id=1, source_target_pairs={{0,8},{1,9},{2,10},{3,11},{4,12},{5,13},{6,14},{7,15},{8,0},{9,1},... | collective-permute-start | bytes 165896 | tf_op jit(solution)/shard_map/ppermute | solution.py:33
  109.1 14.9 %collective-permute-start.22 = (f32[3,1,18,128]{3,2,0,1:T(8,128)}, f32[3,1,18,128]{3,2,0,1:T(8,128)}, u32[]{:S(2)}, u32[]{:S(2)}) collective-permute-start(f32[3,1,18,128]{3,2,0,1:T(8,128)} %get-tuple-element.44), channel_id=1, source_target_pairs={{0,16},{16,32},{32,48},{48,64},{64,80},{80,96},{96,112},{112,128},... | collective-permute-start | bytes 82952 | tf_op jit(solution)/shard_map/ppermute | solution.py:23
  120.9 6.5 %collective-permute-start.23 = (f32[3,1,18,128]{3,2,0,1:T(8,128)}, f32[3,1,18,128]{3,2,0,1:T(8,128)}, u32[]{:S(2)}, u32[]{:S(2)}) collective-permute-start(f32[3,1,18,128]{3,2,0,1:T(8,128)} %get-tuple-element.45), channel_id=1, source_target_pairs={{16,0},{32,16},{48,32},{64,48},{80,64},{96,80},{112,96},{128,112},... | collective-permute-start | bytes 82952 | tf_op jit(solution)/shard_map/ppermute | solution.py:25
  131.1 0.9 copy-start.7
  131.1 1.0 copy-start.9
  131.1 1.0 copy-start.11
  131.1 1.1 copy-start.13
  131.1 1.1 copy-start.15
  132.3 1.0 copy-start.4
  132.3 1.1 copy-start.5
  132.3 1.1 copy-start.16
  132.3 1.2 copy-start.17
  132.3 1.2 copy-start.18
where the time goes:
time: 135 us
  starting transfers between devices  70.2 us (52%)
  waiting for transfers between devices  38.5 us (29%)
  other arithmetic  15.8 us (12%)
  local copies, waits for them, and re-layouts  7.07 us (5%)
  matrix products  1.87 us (1%)
    ppermute x12, waiting for transfers between devices, partner_2(): lax.ppermute(array, axis, [(i, i ^ 1 << apart) for i in range(lax.axis_si...  33.9 us
    ppermute x6, starting transfers between devices, padded_2(): lax.ppermute(tail, axis, [(i, (i + 1) % count) for i in range(ends)])  30.8 us
    ppermute x6, starting transfers between devices, padded_2(): lax.ppermute(head, axis, [((i + 1) % count, i) for i in range(ends)])  20.3 us
    ppermute x12, starting transfers between devices, partner_2(): lax.ppermute(array, axis, [(i, i ^ 1 << apart) for i in range(lax.axis_si...  19.1 us
    unnamed x55, local copies, waits for them, and re-layouts  4.14 us
    ppermute x6, waiting for transfers between devices, padded_2(): lax.ppermute(head, axis, [((i + 1) % count, i) for i in range(ends)])  3.35 us
  transfers between devices with their start and end apart: 24, of which 11 were waited for; matrix products, arithmetic and copies ran while one was open for 4% of the time, Pallas kernels for 0%

commit v1 on v0

v1 whole, which is shorter than its diff:
```python
import functools

import jax
import jax.numpy as jnp
from jax import lax
from jax.experimental import pallas as pl
from jax.experimental.pallas import tpu as pltpu
from jax.sharding import PartitionSpec as P

SEGS = 16
MESH = pl.DeviceIdType.MESH
f32 = jnp.float32

theta_value = 1.025
delta_value = 0.975
sigma_value = theta_value / delta_value
rho_first = 1.0 / sigma_value
rho_second = 1.0 / (2.0 * sigma_value - rho_first)

W = 16
ROWS = W + 6
RING = W + 8
HI, LO, MIRROR = W + 2, 0, W + 4


def routes(gx, gy):
    nx, ny = lax.axis_size("gx"), lax.axis_size("gy")
    first, last = gx == 0, gx == nx - 1
    xl = jnp.where(first, 0, gx - 1)
    xh = jnp.where(last, nx - 1, gx + 1)
    down, up = lax.rem(gy + ny - 1, ny), lax.rem(gy + 1, ny)
    mid = ny - 1 - gy
    mid_down, mid_up = lax.rem(mid + ny - 1, ny), lax.rem(mid + 1, ny)
    pick = jnp.where
    return [
        ((gx, down), 1),
        ((gx, up), 0),
        ((xl, pick(first, mid, gy)), pick(first, 2, 3)),
        ((xh, pick(last, mid, gy)), pick(last, 3, 2)),
        ((xl, pick(first, mid_up, down)), pick(first, 4, 7)),
        ((xl, pick(first, mid_down, up)), pick(first, 5, 6)),
        ((xh, pick(last, mid_up, down)), pick(last, 6, 5)),
        ((xh, pick(last, mid_down, up)), pick(last, 7, 4)),
    ]


def pieces(width, first, last):
    xs_lo, xs_hi = pl.ds(0, width), pl.ds(W - width, width)
    whole = pl.ds(0, W)
    to_lo = jnp.where(first, MIRROR, HI)
    to_hi = jnp.where(last, MIRROR + 2 - width, LO + 2 - width)
    xd_lo, xd_hi = pl.ds(to_lo, width), pl.ds(to_hi, width)
    yd_lo, yd_hi = pl.ds(W, width), pl.ds(RING - width, width)
    block = pl.ds(2, W)
    return [
        (whole, xs_lo, block, yd_lo),
        (whole, xs_hi, block, yd_hi),
        (xs_lo, whole, xd_lo, whole),
        (xs_hi, whole, xd_hi, whole),
        (xs_lo, xs_lo, xd_lo, yd_lo),
        (xs_lo, xs_hi, xd_lo, yd_hi),
        (xs_hi, xs_lo, xd_hi, yd_lo),
        (xs_hi, xs_hi, xd_hi, yd_hi),
    ]


def sym_apply(c, u):
    return (
        c[0] * u[0] + c[3] * u[1] + c[4] * u[2],
        c[3] * u[0] + c[1] * u[1] + c[5] * u[2],
        c[4] * u[0] + c[5] * u[1] + c[2] * u[2],
    )


def ring_sum(h):
    return (h + h) + (pltpu.roll(h, 1, 0) + pltpu.roll(h, RING - 1, 0))


def depth_sum(h, repeat):
    lane = lax.broadcasted_iota(jnp.int32, h.shape, 1)
    end = h if repeat else jnp.zeros_like(h)
    below = jnp.where(lane == 0, end, pltpu.roll(h, 1, 1))
    above = jnp.where(lane == 127, end, pltpu.roll(h, 127, 1))
    return (h + h) + (below + above)


def kernel(
    load, guess, labels, segments, table, out_u, out_r,
    u_ext, l_ext, k_ext, c_ext, v_ext, d_ext, inv, cs_ext, lab, seg, local_sem, send_sem, recv_sem,
):
    gx, gy = lax.axis_index("gx"), lax.axis_index("gy")
    first, last = gx == 0, gx == lax.axis_size("gx") - 1
    own = (pl.ds(2, W), pl.ds(0, W))
    fetch = [
        pltpu.make_async_copy(labels, lab, local_sem.at[0]),
        pltpu.make_async_copy(segments, seg, local_sem.at[1]),
        pltpu.make_async_copy(guess, u_ext.at[:, *own], local_sem.at[2]),
        pltpu.make_async_copy(load, l_ext.at[:, *own], local_sem.at[3]),
    ]
    for copy in fetch:
        copy.start()
    k_ext[:, W:RING] = jnp.zeros((ROWS, 8, 128), jnp.int32)
    k_ext[0:2, 0:W] = jnp.zeros((2, W, 128), jnp.int32)
    k_ext[HI:ROWS, 0:W] = jnp.zeros((4, W, 128), jnp.int32)

    to = routes(gx, gy)
    here = [None] * 4 + [jnp.logical_and(d[0] == gx, d[1] == gy) for d, _ in to[4:]]
    barrier = pltpu.get_barrier_semaphore()
    expected = 4
    for (device, _), same in zip(to, here):
        if same is None:
            pl.semaphore_signal(barrier, inc=1, device_id=device, device_id_type=MESH)
        else:

            @pl.when(jnp.logical_not(same))
            def _():
                pl.semaphore_signal(barrier, inc=1, device_id=device, device_id_type=MESH)

            expected = expected + jnp.where(same, 0, 1)
    pl.semaphore_wait(barrier, expected)

    def view(ref, x, y):
        return ref.at[:, x, y] if len(ref.shape) == 4 else ref.at[x, y]

    def send(kind, src, dst, width, shift):
        copies = []
        for n, (xs, ys, xd, yd) in enumerate(pieces(width, first, last)):
            device, slot = to[n]
            source = view(src, pl.ds(xs.start + shift, xs.size), ys)
            target = view(dst, xd, yd)
            copy = pltpu.make_async_remote_copy(
                src_ref=source,
                dst_ref=target,
                send_sem=send_sem.at[kind, n],
                recv_sem=recv_sem.at[kind, slot],
                device_id=device,
                device_id_type=MESH,
            )
            if here[n] is None:
                copy.start()
            else:
                local = pltpu.make_async_copy(source, target, recv_sem.at[kind, slot])
                pl.when(jnp.logical_not(here[n]))(copy.start)
                pl.when(here[n])(local.start)
            copies.append(copy)
        return copies

    def receive(kind, dst, width):
        whole, block = pl.ds(0, W), pl.ds(2, W)
        xr, yr = pl.ds(0, width), pl.ds(W, width)
        for slot in range(8):
            part = (block, yr) if slot < 2 else (xr, whole) if slot < 4 else (xr, yr)
            ref = view(dst, *part)
            pltpu.make_async_copy(ref, ref, recv_sem.at[kind, slot]).wait()

    sent = send(0, guess, u_ext, 2, 0)
    fetch[0].wait()
    fetch[1].wait()
    k_ext[2:HI, 0:W] = lab[...] * SEGS + seg[...]
    sent += send(1, k_ext, k_ext, 2, 2)
    sent += send(2, load, l_ext, 1, 0)
    fetch[2].wait()
    fetch[3].wait()

    def lookup(x, rows, size, sign):
        codes = k_ext[x, pl.ds(rows, size)]
        for entry in range(6):
            line = jnp.broadcast_to(table[entry : entry + 1, :], (size, 128))
            value = jnp.take_along_axis(line, codes, axis=1, mode="promise_in_bounds")
            if entry >= 4 and sign is not None:
                value = value * sign
            c_ext[entry, x, pl.ds(rows, size)] = value

    @pl.loop(2, HI)
    def _(x):
        lookup(x, 0, W, None)

    receive(0, u_ext, 2)
    receive(1, k_ext, 2)
    receive(2, l_ext, 1)

    turn = 7 - lax.broadcasted_iota(jnp.int32, (8, 128), 0)

    def turned(tile):
        return jnp.take_along_axis(tile, turn, axis=0, mode="promise_in_bounds")

    @pl.when(jnp.logical_or(first, last))
    def _():
        base = jnp.where(first, LO, HI)
        for j in range(2):
            for to_tile, from_tile in ((0, 1), (1, 0), (2, 2)):
                dst, src = pl.ds(8 * to_tile, 8), pl.ds(8 * from_tile, 8)
                k_ext[base + j, dst] = turned(k_ext[MIRROR + 1 - j, src])
                for c, s in enumerate((-1.0, -1.0, 1.0)):
                    u_ext[c, base + j, dst] = s * turned(u_ext[c, MIRROR + 1 - j, src])
                    l_ext[c, base + j, dst] = s * turned(l_ext[c, MIRROR + 1 - j, src])

    @pl.loop(2, HI)
    def _(x):
        lookup(x, W, 8, None)

    low_sign = jnp.where(first, -1.0, 1.0)
    high_sign = jnp.where(last, -1.0, 1.0)
    for x, sign in ((0, low_sign), (1, low_sign), (HI, high_sign), (HI + 1, high_sign)):
        lookup(x, 0, RING, sign)

    @pl.loop(0, W + 4)
    def _(x):
        v = sym_apply([c_ext[e, x] for e in range(6)], [u_ext[c, x] for c in range(3)])
        for c in range(3):
            v_ext[c, x] = v[c]

    def rows_sum(ref, e, x):
        return (ref[e, x - 1] + ref[e, x + 1]) + 2.0 * ref[e, x]

    @pl.loop(1, W + 3)
    def _(x):
        c = [c_ext[e, x] for e in range(6)]
        u = [u_ext[k, x] for k in range(3)]
        c_sum = [depth_sum(ring_sum(rows_sum(c_ext, e, x)), True) for e in range(6)]
        u_sum = [depth_sum(ring_sum(rows_sum(u_ext, k, x)), False) for k in range(3)]
        v_sum = [depth_sum(ring_sum(rows_sum(v_ext, k, x)), False) for k in range(3)]
        near = sym_apply(c, [64.0 * u[k] - u_sum[k] for k in range(3)])
        far = sym_apply(c_sum, u)
        for k in range(3):
            r = l_ext[k, x] - 0.0625 * (near[k] + far[k] - v_sum[k])
            inverse = 16.0 / (48.0 * c[k] + c_sum[k])
            d_ext[k, x] = u[k] + (inverse * r) * (1.0 / theta_value)
            inv[k, x] = inverse
        for e in range(6):
            cs_ext[e, x] = c_sum[e]

    @pl.loop(1, W + 3)
    def _(x):
        v = sym_apply([c_ext[e, x] for e in range(6)], [d_ext[k, x] for k in range(3)])
        for k in range(3):
            v_ext[k, x] = v[k]

    @pl.loop(2, HI)
    def _(x):
        c = [c_ext[e, x, 0:W] for e in range(6)]
        c_sum = [cs_ext[e, x, 0:W] for e in range(6)]
        d = [d_ext[k, x, 0:W] for k in range(3)]
        u_sum = [depth_sum(ring_sum(rows_sum(d_ext, k, x))[0:W], False) for k in range(3)]
        v_sum = [depth_sum(ring_sum(rows_sum(v_ext, k, x))[0:W], False) for k in range(3)]
        near = sym_apply(c, [64.0 * d[k] - u_sum[k] for k in range(3)])
        far = sym_apply(c_sum, d)
        for k in range(3):
            r = l_ext[k, x, 0:W] - 0.0625 * (near[k] + far[k] - v_sum[k])
            step = d[k] - u_ext[k, x, 0:W]
            step = (rho_second * rho_first) * step + (2.0 * rho_second / delta_value) * inv[k, x, 0:W] * r
            out_u[k, x - 2] = d[k] + step
            out_r[k, x - 2] = r

    for n, copy in enumerate(sent):
        if here[n % 8] is None:
            copy.wait_send()
        else:
            pl.when(jnp.logical_not(here[n % 8]))(copy.wait_send)


def write(u, r, out_u, out_r, sem):
    copies = [
        pltpu.make_async_copy(u, out_u, sem.at[0]),
        pltpu.make_async_copy(r, out_r, sem.at[1]),
    ]
    for copy in copies:
        copy.start()
    for copy in copies:
        copy.wait()


def body(load, guess, labels, segments, stiffness):
    table = jnp.pad(stiffness, ((0, 2), (0, 128 - stiffness.shape[1])))
    vmem = pl.BlockSpec(memory_space=pltpu.VMEM)
    anywhere = pl.BlockSpec(memory_space=pl.ANY)
    shape = load.shape
    wide = (ROWS, RING, 128)
    results = pl.pallas_call(
        kernel,
        out_shape=[pltpu.VMEM(shape, f32)] * 2,
        in_specs=[anywhere] * 4 + [vmem],
        out_specs=[vmem] * 2,
        scratch_shapes=[
            pltpu.VMEM((3,) + wide, f32),
            pltpu.VMEM((3,) + wide, f32),
            pltpu.VMEM(wide, jnp.int32),
            pltpu.VMEM((6,) + wide, f32),
            pltpu.VMEM((3,) + wide, f32),
            pltpu.VMEM((3,) + wide, f32),
            pltpu.VMEM((3,) + wide, f32),
            pltpu.VMEM((6,) + wide, f32),
            pltpu.VMEM((W, W, 128), jnp.int32),
            pltpu.VMEM((W, W, 128), jnp.int32),
            pltpu.SemaphoreType.DMA((4,)),
            pltpu.SemaphoreType.DMA((3, 8)),
            pltpu.SemaphoreType.DMA((3, 8)),
        ],
        compiler_params=pltpu.CompilerParams(
            collective_id=0, has_side_effects=True, vmem_limit_bytes=40 * 2**20
        ),
    )(load, guess, labels, segments, table)
    results = [pltpu.with_memory_space_constraint(x, pltpu.VMEM) for x in results]
    return tuple(
        pl.pallas_call(
            write,
            out_shape=[jax.ShapeDtypeStruct(shape, f32)] * 2,
            in_specs=[vmem] * 2,
            out_specs=[anywhere] * 2,
            scratch_shapes=[pltpu.SemaphoreType.DMA((2,))],
        )(*results)
    )


def solution(mesh):
    field = P(None, "gx", "gy", None)
    voxel = P("gx", "gy", None)
    return jax.shard_map(
        body,
        mesh=mesh,
        in_specs=(field, field, voxel, voxel, P()),
        out_specs=(field, field),
        check_vma=False,
    )
```

time: 135 us -> 32.3 us (0.24)
  the two profiles are of different devices: /device:TPU:49 before, /device:TPU:1 now
where the time goes in v1:
time: 32.3 us; the launch traced here: 32 us
  Pallas kernels  26.9 us (83%)
  local copies, waits for them, and re-layouts  4.49 us (14%)
  between operations  0.64 us (2%)
    pallas_call x1, Pallas kernels, body(): pl.pallas_call(kernel, out_shape=[pltpu.VMEM(shape, f32)] * 2, in_specs=[...  26 us
    unnamed x8, local copies, waits for them, and re-layouts  3.8 us
    pallas_call x1, Pallas kernels, body(): pl.pallas_call(write, out_shape=[jax.ShapeDtypeStruct(shape, f32)] * 2, i...  0.89 us
    pad x1, local copies, waits for them, and re-layouts, body(): table = jnp.pad(stiffness, ((0, 2), (0, 128 - stiffness.shape[1])))  0.69 us

profile of v1, /device:TPU:1, one launch (start us, length us, event | category | flops | bytes accessed | tf_op | source)
XLA Modules:
  0.0 32.0 jit_solution(425619426450089196)
XLA Ops:
  0.6 0.7 %pad.4.table = f32[8,128]{1,0:T(8,128)S(1)} pad(f32[6,48]{1,0:T(8,128)} %param.9, f32[]{:T(128)} %constant.2.clone.1), padding=0_2x0_80 | pad | bytes 5252 | tf_op jit(solution)/shard_map/jit(_pad)/pad | solution.py:274
  1.3 0.0 copy-start
  1.3 1.0 %copy-done = f32[3,16,16,128]{3,2,1,0:T(8,128)S(1)} copy-done((f32[3,16,16,128]{3,2,1,0:T(8,128)S(1)}, f32[3,16,16,128]{3,2,1,0:T(8,128)}, u32[]{:S(2)}) %copy-start) | copy-done | bytes 393240
  2.3 0.0 copy-start.1
  2.3 1.0 %copy-done.1 = f32[3,16,16,128]{3,2,1,0:T(8,128)S(1)} copy-done((f32[3,16,16,128]{3,2,1,0:T(8,128)S(1)}, f32[3,16,16,128]{3,2,1,0:T(8,128)}, u32[]{:S(2)}) %copy-start.1) | copy-done | bytes 393240
  3.3 0.0 copy-start.2
  3.3 0.9 %copy-done.2 = s32[16,16,128]{2,1,0:T(8,128)S(1)} copy-done((s32[16,16,128]{2,1,0:T(8,128)S(1)}, s32[16,16,128]{2,1,0:T(8,128)}, u32[]{:S(2)}) %copy-start.2) | copy-done | bytes 131096
  4.2 0.0 copy-start.3
  4.2 0.9 %copy-done.3 = s32[16,16,128]{2,1,0:T(8,128)S(1)} copy-done((s32[16,16,128]{2,1,0:T(8,128)S(1)}, s32[16,16,128]{2,1,0:T(8,128)}, u32[]{:S(2)}) %copy-start.3) | copy-done | bytes 131096
  5.1 26.0 %shard_map.68 = (f32[3,16,16,128]{3,2,1,0:T(8,128)S(1)}, f32[3,16,16,128]{3,2,1,0:T(8,128)S(1)}) custom-call(f32[3,16,16,128]{3,2,1,0:T(8,128)S(1)} %copy-done, f32[3,16,16,128]{3,2,1,0:T(8,128)S(1)} %copy-done.1, s32[16,16,128]{2,1,0:T(8,128)S(1)} %copy-done.2, s32[16,16,128]{2,1,0:T(8,128)S(1)} %copy-done.3, f32[8,128]{1,0:T(8,128)S(1)} %pad.4.table), custom_call_target="tpu_custom_call" | custom-call | tf_op jit(solution)/shard_map/pallas_call | solution.py:279
  31.1 0.9 %shard_map.69 = (f32[3,16,16,128]{3,2,1,0:T(8,128)}, f32[3,16,16,128]{3,2,1,0:T(8,128)}) custom-call(f32[3,16,16,128]{3,2,1,0:T(8,128)S(1)} %get-tuple-element.4.u, f32[3,16,16,128]{3,2,1,0:T(8,128)S(1)} %get-tuple-element.5.r), custom_call_target="tpu_custom_call" | custom-call | tf_op jit(solution)/shard_map/pallas_call | solution.py:305
Async XLA Ops:
  1.3 1.0 %copy-start = (f32[3,16,16,128]{3,2,1,0:T(8,128)S(1)}, f32[3,16,16,128]{3,2,1,0:T(8,128)}, u32[]{:S(2)}) copy-start(f32[3,16,16,128]{3,2,1,0:T(8,128)} %load.1) | copy-start | bytes 1179652
  2.3 1.0 %copy-start.1 = (f32[3,16,16,128]{3,2,1,0:T(8,128)S(1)}, f32[3,16,16,128]{3,2,1,0:T(8,128)}, u32[]{:S(2)}) copy-start(f32[3,16,16,128]{3,2,1,0:T(8,128)} %guess.1) | copy-start | bytes 1179652
  3.3 0.9 %copy-start.2 = (s32[16,16,128]{2,1,0:T(8,128)S(1)}, s32[16,16,128]{2,1,0:T(8,128)}, u32[]{:S(2)}) copy-start(s32[16,16,128]{2,1,0:T(8,128)} %labels.1) | copy-start | bytes 393220
  4.2 0.9 %copy-start.3 = (s32[16,16,128]{2,1,0:T(8,128)S(1)}, s32[16,16,128]{2,1,0:T(8,128)}, u32[]{:S(2)}) copy-start(s32[16,16,128]{2,1,0:T(8,128)} %segments.1) | copy-start | bytes 393220

commit v2 on v1

--- a/solution.py
+++ b/solution.py
@@ -85,8 +85,8 @@
 
 
 def kernel(
-    load, guess, labels, segments, table, out_u, out_r,
-    u_ext, l_ext, k_ext, c_ext, v_ext, d_ext, inv, cs_ext, lab, seg, local_sem, send_sem, recv_sem,
+    load, guess, labels, segments, stiffness, out_u, out_r,
+    blocks, table, u_ext, l_ext, k_ext, c_ext, v_ext, d_ext, inv, cs_ext, lab, seg, local_sem, send_sem, recv_sem,
 ):
     gx, gy = lax.axis_index("gx"), lax.axis_index("gy")
     first, last = gx == 0, gx == lax.axis_size("gx") - 1
@@ -96,6 +96,7 @@
         pltpu.make_async_copy(segments, seg, local_sem.at[1]),
         pltpu.make_async_copy(guess, u_ext.at[:, *own], local_sem.at[2]),
         pltpu.make_async_copy(load, l_ext.at[:, *own], local_sem.at[3]),
+        pltpu.make_async_copy(stiffness, blocks, local_sem.at[4]),
     ]
     for copy in fetch:
         copy.start()
@@ -161,6 +162,8 @@
     sent += send(2, load, l_ext, 1, 0)
     fetch[2].wait()
     fetch[3].wait()
+    fetch[4].wait()
+    table[0:6, 0 : stiffness.shape[1]] = blocks[...]
 
     def lookup(x, rows, size, sign):
         codes = k_ext[x, pl.ds(rows, size)]
@@ -271,17 +274,19 @@
 
 
 def body(load, guess, labels, segments, stiffness):
-    table = jnp.pad(stiffness, ((0, 2), (0, 128 - stiffness.shape[1])))
     vmem = pl.BlockSpec(memory_space=pltpu.VMEM)
     anywhere = pl.BlockSpec(memory_space=pl.ANY)
+    hbm = pl.BlockSpec(memory_space=pltpu.HBM)
     shape = load.shape
     wide = (ROWS, RING, 128)
     results = pl.pallas_call(
         kernel,
         out_shape=[pltpu.VMEM(shape, f32)] * 2,
-        in_specs=[anywhere] * 4 + [vmem],
+        in_specs=[hbm] * 5,
         out_specs=[vmem] * 2,
         scratch_shapes=[
+            pltpu.VMEM(stiffness.shape, f32),
+            pltpu.VMEM((8, 128), f32),
             pltpu.VMEM((3,) + wide, f32),
             pltpu.VMEM((3,) + wide, f32),
             pltpu.VMEM(wide, jnp.int32),
@@ -292,14 +297,14 @@
             pltpu.VMEM((6,) + wide, f32),
             pltpu.VMEM((W, W, 128), jnp.int32),
             pltpu.VMEM((W, W, 128), jnp.int32),
-            pltpu.SemaphoreType.DMA((4,)),
+            pltpu.SemaphoreType.DMA((5,)),
             pltpu.SemaphoreType.DMA((3, 8)),
             pltpu.SemaphoreType.DMA((3, 8)),
         ],
         compiler_params=pltpu.CompilerParams(
             collective_id=0, has_side_effects=True, vmem_limit_bytes=40 * 2**20
         ),
-    )(load, guess, labels, segments, table)
+    )(*[pltpu.with_memory_space_constraint(x, pltpu.HBM) for x in (load, guess, labels, segments, stiffness)])
     results = [pltpu.with_memory_space_constraint(x, pltpu.VMEM) for x in results]
     return tuple(
         pl.pallas_call(

time: 32.3 us -> 27.7 us (0.86)
  local copies, waits for them, and re-layouts: 4.49 us -> 0 us
    unnamed x8 -> x0, local copies, waits for them, and re-layouts: 3.8 us -> none
    pad x1 -> x0, local copies, waits for them, and re-layouts: 0.69 us -> none  [body(): table = jnp.pad(stiffness, ((0, 2), (0, 128 - stiffness.shape[1])))]
where the time goes in v2:
time: 27.7 us; the launch traced here: 27.6 us
  Pallas kernels  26.9 us (97%)
  between operations  0.64 us (2%)
    pallas_call x1, Pallas kernels, body(): pl.pallas_call(kernel, out_shape=[pltpu.VMEM(shape, f32)] * 2, in_specs=[...  26 us
    pallas_call x1, Pallas kernels, body(): pl.pallas_call(write, out_shape=[jax.ShapeDtypeStruct(shape, f32)] * 2, i...  0.89 us

profile of v2, /device:TPU:1, one launch (start us, length us, event | category | flops | bytes accessed | tf_op | source)
XLA Modules:
  0.0 27.6 jit_solution(8682882431418668852)
XLA Ops:
  0.6 26.0 %shard_map.68 = (f32[3,16,16,128]{3,2,1,0:T(8,128)S(1)}, f32[3,16,16,128]{3,2,1,0:T(8,128)S(1)}) custom-call(f32[3,16,16,128]{3,2,1,0:T(8,128)} %load.1, f32[3,16,16,128]{3,2,1,0:T(8,128)} %guess.1, s32[16,16,128]{2,1,0:T(8,128)} %labels.1, s32[16,16,128]{2,1,0:T(8,128)} %segments.1, f32[6,48]{1,0:T(8,128)} %stiffness.1), custom_call_target="tpu_custom_call" | custom-call | tf_op jit(solution)/shard_map/pallas_call | solution.py:282
  26.7 0.9 %shard_map.69 = (f32[3,16,16,128]{3,2,1,0:T(8,128)}, f32[3,16,16,128]{3,2,1,0:T(8,128)}) custom-call(f32[3,16,16,128]{3,2,1,0:T(8,128)S(1)} %get-tuple-element.4.u, f32[3,16,16,128]{3,2,1,0:T(8,128)S(1)} %get-tuple-element.5.r), custom_call_target="tpu_custom_call" | custom-call | tf_op jit(solution)/shard_map/pallas_call | solution.py:310

commit v3 on v2

v3 whole, which is shorter than its diff:
```python
import functools

import jax
import jax.numpy as jnp
from jax import lax
from jax.experimental import pallas as pl
from jax.experimental.pallas import tpu as pltpu
from jax.sharding import PartitionSpec as P

SEGS = 16
MESH = pl.DeviceIdType.MESH
f32 = jnp.float32

theta_value = 1.025
delta_value = 0.975
sigma_value = theta_value / delta_value
rho_first = 1.0 / sigma_value
rho_second = 1.0 / (2.0 * sigma_value - rho_first)

W = 16
RING = W + 8
VALUES = 11
EARLY = 8
SIGNS = (-1.0, -1.0, 1.0) * 2 + (1.0, 1.0) + (-1.0, -1.0, 1.0)


def routes(gx, gy):
    nx, ny = lax.axis_size("gx"), lax.axis_size("gy")
    first, last = gx == 0, gx == nx - 1
    xl = jnp.where(first, 0, gx - 1)
    xh = jnp.where(last, nx - 1, gx + 1)
    down, up = lax.rem(gy + ny - 1, ny), lax.rem(gy + 1, ny)
    mid = ny - 1 - gy
    mid_down, mid_up = lax.rem(mid + ny - 1, ny), lax.rem(mid + 1, ny)
    pick = jnp.where
    return [
        ((gx, down), 1),
        ((gx, up), 0),
        ((xl, pick(first, mid, gy)), pick(first, 2, 3)),
        ((xh, pick(last, mid, gy)), pick(last, 3, 2)),
        ((xl, pick(first, mid_up, down)), (7, 4)),
        ((xl, pick(first, mid_down, up)), (6, 5)),
        ((xh, pick(last, mid_up, down)), (5, 6)),
        ((xh, pick(last, mid_down, up)), (4, 7)),
    ]


def sym_apply(c, u):
    return (
        c[0] * u[0] + c[3] * u[1] + c[4] * u[2],
        c[3] * u[0] + c[1] * u[1] + c[5] * u[2],
        c[4] * u[0] + c[5] * u[1] + c[2] * u[2],
    )


def along_row(h):
    n = h.shape[0]
    return (h + h) + (pltpu.roll(h, 1, 0) + pltpu.roll(h, n - 1, 0))


def along_depth(h, repeat=False):
    lane = lax.broadcasted_iota(jnp.int32, h.shape, 1)
    end = h if repeat else jnp.zeros_like(h)
    below = jnp.where(lane == 0, end, pltpu.roll(h, 1, 1))
    above = jnp.where(lane == 127, end, pltpu.roll(h, 127, 1))
    return (h + h) + (below + above)


def weigh(h, repeat=False):
    return along_depth(along_row(h), repeat)


def line(x):
    return pl.ds(W * x, W) if isinstance(x, int) else pl.ds(pl.multiple_of(W * x, W), W)


def kernel(
    load, guess, labels, segments, stiffness, u_own, r_own, d_own, inv_own,
    blocks, table, l_own, k_own, lab, seg, c_own, v_own, cs_own, snd, rcv, t2g, t2o, c_strip,
    local_sem, send_sem, late_send_sem, recv_sem, late_recv_sem,
):
    gx, gy = lax.axis_index("gx"), lax.axis_index("gy")
    first, last = gx == 0, gx == lax.axis_size("gx") - 1
    fetch = [
        pltpu.make_async_copy(labels, lab, local_sem.at[0]),
        pltpu.make_async_copy(segments, seg, local_sem.at[1]),
        pltpu.make_async_copy(guess, u_own, local_sem.at[2]),
        pltpu.make_async_copy(load, l_own, local_sem.at[3]),
        pltpu.make_async_copy(stiffness, blocks, local_sem.at[4]),
    ]
    for copy in fetch:
        copy.start()
    t2g[...] = jnp.zeros(t2g.shape, f32)

    to = routes(gx, gy)
    here = [None] * 4 + [jnp.logical_and(d[0] == gx, d[1] == gy) for d, _ in to[4:]]
    barrier = pltpu.get_barrier_semaphore()
    expected = 4
    for (device, _), same in zip(to, here):
        if same is None:
            pl.semaphore_signal(barrier, inc=1, device_id=device, device_id_type=MESH)
        else:

            @pl.when(jnp.logical_not(same))
            def _():
                pl.semaphore_signal(barrier, inc=1, device_id=device, device_id_type=MESH)

            expected = expected + jnp.where(same, 0, 1)

    t2o[...] = jnp.zeros(t2o.shape, f32)
    fetch[0].wait()
    fetch[1].wait()
    k_own[...] = (lab[...] * SEGS + seg[...]).astype(f32)
    fetch[2].wait()
    fetch[3].wait()
    sides = ((0, 1), (W - 1, W - 2))
    for s in range(4):
        for j in range(2):
            at = sides[s % 2][j]
            rows = pl.ds(at, W, stride=W) if s < 2 else line(at)
            for c in range(3):
                snd[s, 3 * j + c] = u_own[c, rows]
                if j == 0:
                    snd[s, EARLY + c] = l_own[c, rows]
            snd[s, 6 + j] = k_own[rows]
    fetch[4].wait()
    table[0:6, 0 : stiffness.shape[1]] = blocks[...]

    pl.semaphore_wait(barrier, expected)

    sent = []

    def send_edge(n, values, out_sem, in_sem):
        device, slot = to[n]
        copy = pltpu.make_async_remote_copy(
            src_ref=snd.at[n, values],
            dst_ref=rcv.at[slot, values],
            send_sem=out_sem.at[n],
            recv_sem=in_sem.at[slot],
            device_id=device,
            device_id_type=MESH,
        )
        copy.start()
        sent.append((copy, None))

    def corner_ref(slot):
        return t2g.at[slot % 2, :, pl.ds(6 if slot < 6 else 0, 2)]

    def send_corner(n):
        device, slots = to[n]
        mirrored = first if n < 6 else last
        source = snd.at[n % 2, :, pl.ds(0 if n < 6 else W - 2, 2)]
        for slot, chosen in zip(slots, (jnp.logical_not(mirrored), mirrored)):
            copy = pltpu.make_async_remote_copy(
                src_ref=source,
                dst_ref=corner_ref(slot),
                send_sem=send_sem.at[n],
                recv_sem=recv_sem.at[slot],
                device_id=device,
                device_id_type=MESH,
            )
            pl.when(jnp.logical_and(chosen, jnp.logical_not(here[n])))(copy.start)
            if slot == slots[1]:
                local = pltpu.make_async_copy(source, corner_ref(slot), recv_sem.at[slot])
                pl.when(jnp.logical_and(chosen, here[n]))(local.start)
        sent.append((copy, here[n]))

    early, late = pl.ds(0, EARLY), pl.ds(EARLY, VALUES - EARLY)
    for n in range(2):
        send_edge(n, early, send_sem, recv_sem)
    for n in range(4, 8):
        send_corner(n)
    for n in range(2, 4):
        send_edge(n, early, send_sem, recv_sem)
    for n in range(4):
        send_edge(n, late, late_send_sem, late_recv_sem)

    def receive(ref, sem):
        pltpu.make_async_copy(ref, ref, sem).wait()

    def lookup(codes, entry):
        rows = jnp.broadcast_to(table[entry : entry + 1, :], codes.shape)
        return jnp.take_along_axis(rows, codes, axis=1, mode="promise_in_bounds")

    inner_row = lax.broadcasted_iota(jnp.int32, (W, 128), 0)
    inner_row = jnp.logical_and(inner_row > 0, inner_row < W - 1)
    none = jnp.zeros((W, 128), f32)
    for x in (0, W - 1):
        for c in range(3):
            d_own[c, line(x)] = none
        for e in range(6):
            cs_own[e, line(x)] = none

    @pl.loop(0, W, unroll=4)
    def _(x):
        codes = k_own[line(x)].astype(jnp.int32)
        c = [lookup(codes, e) for e in range(6)]
        for e in range(6):
            c_own[e, line(x)] = c[e]
        v = sym_apply(c, [u_own[k, line(x)] for k in range(3)])
        for k in range(3):
            v_own[k, line(x)] = v[k]

    for s in range(4):
        for j in range(2):
            codes = snd[s, 6 + j].astype(jnp.int32)
            for e in range(6):
                c_strip[s, 2 + j, e, 0:W] = lookup(codes, e)

    def three(ref, e, x):
        return (ref[e, line(x - 1)] + ref[e, line(x + 1)]) + 2.0 * ref[e, line(x)]

    @pl.loop(1, W - 1, unroll=2)
    def _(x):
        c = [c_own[e, line(x)] for e in range(6)]
        u = [u_own[k, line(x)] for k in range(3)]
        c_sum = [weigh(three(c_own, e, x), True) for e in range(6)]
        u_sum = [weigh(three(u_own, k, x)) for k in range(3)]
        v_sum = [weigh(three(v_own, k, x)) for k in range(3)]
        near = sym_apply(c, [64.0 * u[k] - u_sum[k] for k in range(3)])
        far = sym_apply(c_sum, u)
        for k in range(3):
            r = l_own[k, line(x)] - 0.0625 * (near[k] + far[k] - v_sum[k])
            inverse = 16.0 / (48.0 * c[k] + c_sum[k])
            d = u[k] + (inverse * r) * (1.0 / theta_value)
            inv_own[k, line(x)] = inverse
            d_own[k, line(x)] = jnp.where(inner_row, d, 0.0)
        for e in range(6):
            cs_own[e, line(x)] = c_sum[e]

    @pl.loop(0, W, unroll=4)
    def _(x):
        v = sym_apply([c_own[e, line(x)] for e in range(6)], [d_own[k, line(x)] for k in range(3)])
        for k in range(3):
            v_own[k, line(x)] = v[k]

    def three_within(ref, e, x):
        below, above = jnp.maximum(x - 1, 0), jnp.minimum(x + 1, W - 1)
        return (ref[e, line(below)] + ref[e, line(above)]) + 2.0 * ref[e, line(x)]

    @pl.loop(0, W, unroll=2)
    def _(x):
        c = [c_own[e, line(x)] for e in range(6)]
        c_sum = [cs_own[e, line(x)] for e in range(6)]
        d = [d_own[k, line(x)] for k in range(3)]
        d_sum = [weigh(three_within(d_own, k, x)) for k in range(3)]
        v_sum = [weigh(three_within(v_own, k, x)) for k in range(3)]
        near = sym_apply(c, [64.0 * d[k] - d_sum[k] for k in range(3)])
        far = sym_apply(c_sum, d)
        for k in range(3):
            r_own[k, line(x)] = l_own[k, line(x)] - 0.0625 * (near[k] + far[k] - v_sum[k])

    turn = 7 - lax.broadcasted_iota(jnp.int32, (8, 128), 0)

    def turned(tile):
        return jnp.take_along_axis(tile, turn, axis=0, mode="promise_in_bounds")

    eight = lax.broadcasted_iota(jnp.int32, (8, 128), 0)
    low_sign = jnp.where(first, -1.0, 1.0)
    high_sign = jnp.where(last, -1.0, 1.0)
    end_sign = jnp.where(eight > 5, low_sign, jnp.where(eight < 2, high_sign, 1.0))

    def strip(s):
        ring = s < 2
        n = RING if ring else W

        def value(row, index):
            own = row > 1
            if not ring:
                return (snd if own else rcv)[s, index]
            ends = t2o if own else t2g
            return jnp.concatenate([(snd if own else rcv)[s, index], ends[s, index]], axis=0)

        def layer(row):
            return (1, 0, 0, 1)[row]

        for row in range(4):
            codes = value(row, 6 + layer(row)).astype(jnp.int32)
            if row < 2:
                for e in range(6):
                    entry = lookup(codes[0:W], e)
                    if e > 3 and not ring:
                        entry = entry * (low_sign if s == 2 else high_sign)
                    c_strip[s, row, e, 0:W] = entry
            if ring:
                for e in range(6):
                    entry = lookup(codes[W:RING], e)
                    c_strip[s, row, e, W:RING] = entry * end_sign if e > 3 else entry
        c = [[c_strip[s, row, e, 0:n] for e in range(6)] for row in range(4)]
        u = [[value(row, 3 * layer(row) + k) for k in range(3)] for row in range(4)]
        v = [sym_apply(c[row], u[row]) for row in range(4)]

        def three_rows(f, row, k):
            return (f[row - 1][k] + f[row + 1][k]) + 2.0 * f[row][k]

        part, inverse, c_sum = {}, {}, {}
        for row in (1, 2):
            c_sum[row] = [weigh(three_rows(c, row, e), True) for e in range(6)]
            u_sum = [weigh(three_rows(u, row, k)) for k in range(3)]
            v_sum = [weigh(three_rows(v, row, k)) for k in range(3)]
            near = sym_apply(c[row], [64.0 * u[row][k] - u_sum[k] for k in range(3)])
            far = sym_apply(c_sum[row], u[row])
            part[row] = [0.0625 * (near[k] + far[k] - v_sum[k]) for k in range(3)]
            inverse[row] = [16.0 / (48.0 * c[row][k] + c_sum[row][k]) for k in range(3)]

        receive(rcv.at[s, late], late_recv_sem.at[s])
        if not ring:
            turn_strip(s, range(EARLY, VALUES))
        d = {}
        for row in (1, 2):
            d[row] = []
            for k in range(3):
                r = value(row, EARLY + k) - part[row][k]
                step = u[row][k] + (inverse[row][k] * r) * (1.0 / theta_value)
                d[row].append(step if ring else jnp.where(inner_row, step, 0.0))
        v = {row: sym_apply(c[row], d[row]) for row in (1, 2)}
        d_sum = [weigh(d[1][k] + 2.0 * d[2][k])[0:W] for k in range(3)]
        v_sum = [weigh(v[1][k] + 2.0 * v[2][k])[0:W] for k in range(3)]
        c2 = [t[0:W] for t in c[2]]
        c3 = [t[0:W] for t in c[3]]
        d2 = [t[0:W] for t in d[2]]
        near = sym_apply(c2, [64.0 * d2[k] - d_sum[k] for k in range(3)])
        far = sym_apply([t[0:W] for t in c_sum[2]], d2)
        outer = [near[k] + far[k] - v_sum[k] for k in range(3)]
        d_sum = [weigh(d[2][k])[0:W] for k in range(3)]
        v_sum = [weigh(v[2][k])[0:W] for k in range(3)]
        near = sym_apply(c3, d_sum)
        nearer, farther = sides[s % 2]
        if ring:
            rows_0, rows_1 = pl.ds(nearer, W, stride=W), pl.ds(farther, W, stride=W)
        else:
            rows_0, rows_1 = line(nearer), line(farther)
        for k in range(3):
            r_own[k, rows_0] = r_own[k, rows_0] - 0.0625 * outer[k]
            r_own[k, rows_1] = r_own[k, rows_1] + 0.0625 * (near[k] + v_sum[k])
            d_own[k, rows_0] = d2[k]
            inv_own[k, rows_0] = inverse[2][k][0:W]

    def turn_strip(s, indices):
        @pl.when(first if s == 2 else last)
        def _():
            for i in indices:
                head, tail = rcv[s, i, 0:8], rcv[s, i, 8:W]
                rcv[s, i, 0:8] = SIGNS[i] * turned(tail)
                rcv[s, i, 8:W] = SIGNS[i] * turned(head)

    for s in (2, 3):
        receive(rcv.at[s, early], recv_sem.at[s])
        turn_strip(s, range(EARLY))
        strip(s)

    for s in range(2):
        for j in range(2):
            at = sides[s][j]
            for side, spot in ((2, (7, 6)), (3, (0, 1))):
                for i in range(2):
                    for c in range(3):
                        t2o[s, 3 * j + c, spot[i]] = rcv[side, 3 * i + c, at]
                    t2o[s, 6 + j, spot[i]] = rcv[side, 6 + i, at]
                if j == 0:
                    for c in range(3):
                        t2o[s, EARLY + c, spot[0]] = rcv[side, EARLY + c, at]

    for s in (1, 0):
        receive(rcv.at[s, early], recv_sem.at[s])
        for slot in (4 + s, 6 + s):
            receive(corner_ref(slot), recv_sem.at[slot])
        for mirrored, base in ((first, 6), (last, 0)):

            @pl.when(mirrored)
            def _():
                for i in range(VALUES):
                    one, two = t2g[s, i, base], t2g[s, i, base + 1]
                    t2g[s, i, base] = SIGNS[i] * two
                    t2g[s, i, base + 1] = SIGNS[i] * one

        strip(s)

    for copy, same in sent:
        if same is None:
            copy.wait_send()
        else:
            pl.when(jnp.logical_not(same))(copy.wait_send)


def finish(u, r, d, inv, out_u, out_r, result, sem):
    copies = [pltpu.make_async_copy(r, out_r, sem.at[3])]
    copies[0].start()
    for k in range(3):
        copies.append(pltpu.make_async_copy(result.at[k], out_u.at[k], sem.at[k]))

        @pl.loop(0, W, unroll=8)
        def _(x):
            step = d[k, line(x)] - u[k, line(x)]
            step = (rho_second * rho_first) * step
            step += (2.0 * rho_second / delta_value) * (inv[k, line(x)] * r[k, line(x)])
            result[k, line(x)] = d[k, line(x)] + step

        copies[-1].start()
    for copy in copies:
        copy.wait()


def body(load, guess, labels, segments, stiffness):
    vmem = pl.BlockSpec(memory_space=pltpu.VMEM)
    hbm = pl.BlockSpec(memory_space=pltpu.HBM)
    shape = load.shape
    field = (3, W * W, 128)
    inputs = (
        load.reshape(field),
        guess.reshape(field),
        labels.reshape(field[1:]),
        segments.reshape(field[1:]),
        stiffness,
    )
    results = pl.pallas_call(
        kernel,
        out_shape=[pltpu.VMEM(field, f32)] * 4,
        in_specs=[hbm] * 5,
        out_specs=[vmem] * 4,
        scratch_shapes=[
            pltpu.VMEM(stiffness.shape, f32),
            pltpu.VMEM((8, 128), f32),
            pltpu.VMEM(field, f32),
            pltpu.VMEM(field[1:], f32),
            pltpu.VMEM(field[1:], jnp.int32),
            pltpu.VMEM(field[1:], jnp.int32),
            pltpu.VMEM((6,) + field[1:], f32),
            pltpu.VMEM(field, f32),
            pltpu.VMEM((6,) + field[1:], f32),
            pltpu.VMEM((4, VALUES, W, 128), f32),
            pltpu.VMEM((4, VALUES, W, 128), f32),
            pltpu.VMEM((2, VALUES, 8, 128), f32),
            pltpu.VMEM((2, VALUES, 8, 128), f32),
            pltpu.VMEM((4, 4, 6, RING, 128), f32),
            pltpu.SemaphoreType.DMA((5,)),
            pltpu.SemaphoreType.DMA((8,)),
            pltpu.SemaphoreType.DMA((4,)),
            pltpu.SemaphoreType.DMA((8,)),
            pltpu.SemaphoreType.DMA((4,)),
        ],
        compiler_params=pltpu.CompilerParams(
            collective_id=0, has_side_effects=True, vmem_limit_bytes=40 * 2**20
        ),
    )(*[pltpu.with_memory_space_constraint(x, pltpu.HBM) for x in inputs])
    out_u, out_r = pl.pallas_call(
        finish,
        out_shape=[jax.ShapeDtypeStruct(field, f32)] * 2,
        in_specs=[vmem] * 4,
        out_specs=[hbm] * 2,
        scratch_shapes=[pltpu.VMEM(field, f32), pltpu.SemaphoreType.DMA((4,))],
    )(*[pltpu.with_memory_space_constraint(x, pltpu.VMEM) for x in results])
    return out_u.reshape(shape), out_r.reshape(shape)


def solution(mesh):
    field = P(None, "gx", "gy", None)
    voxel = P("gx", "gy", None)
    return jax.shard_map(
        body,
        mesh=mesh,
        in_specs=(field, field, voxel, voxel, P()),
        out_specs=(field, field),
        check_vma=False,
    )
```

time: 27.7 us -> 21.1 us (0.76)
  the two profiles are of different devices: /device:TPU:1 before, /device:TPU:49 now
where the time goes in v3:
time: 21.1 us; the launch traced here: 21 us
  Pallas kernels  20.4 us (97%)
  between operations  0.64 us (3%)
    pallas_call x1, Pallas kernels, body(): pl.pallas_call(kernel, out_shape=[pltpu.VMEM(field, f32)] * 4, in_specs=[...  19.5 us
    pallas_call x1, Pallas kernels, body(): pl.pallas_call(finish, out_shape=[jax.ShapeDtypeStruct(field, f32)] * 2,...  0.91 us

profile of v3, /device:TPU:49, one launch (start us, length us, event | category | flops | bytes accessed | tf_op | source)
XLA Modules:
  0.0 21.0 jit_solution(13374164919051156755)
XLA Ops:
  0.6 19.5 %shard_map.68 = (f32[3,256,128]{2,1,0:T(8,128)S(1)}, f32[3,256,128]{2,1,0:T(8,128)S(1)}, f32[3,256,128]{2,1,0:T(8,128)S(1)}, f32[3,256,128]{2,1,0:T(8,128)S(1)}) custom-call(f32[3,256,128]{2,1,0:T(8,128)} %bitcast.6, f32[3,256,128]{2,1,0:T(8,128)} %bitcast.7, s32[256,128]{1,0:T(8,128)} %bitcast.8, s32[256,128]{1,0:T(8,128)} %bitcast.9, f32[6,48]{1,0:T(8,128)} %stiffness.1), custom_call_target="tpu_custom_call" | custom-call | tf_op jit(solution)/shard_map/pallas_call | solution.py:416
  20.1 0.9 %shard_map.69 = (f32[3,256,128]{2,1,0:T(8,128)}, f32[3,256,128]{2,1,0:T(8,128)}) custom-call(f32[3,256,128]{2,1,0:T(8,128)S(1)} %get-tuple-element.8.u, f32[3,256,128]{2,1,0:T(8,128)S(1)} %get-tuple-element.9.r, f32[3,256,128]{2,1,0:T(8,128)S(1)} %get-tuple-element.10.d, f32[3,256,128]{2,1,0:T(8,128)S(1)} %get-tuple-element.11.inv), custom_call_target="tpu_custom_call" | custom-call | tf_op jit(solution)/shard_map/pallas_call | solution.py:446

commit v4 on v3

--- a/solution.py
+++ b/solution.py
@@ -128,52 +128,94 @@
 
     pl.semaphore_wait(barrier, expected)
 
-    sent = []
-
-    def send_edge(n, values, out_sem, in_sem):
-        device, slot = to[n]
-        copy = pltpu.make_async_remote_copy(
-            src_ref=snd.at[n, values],
-            dst_ref=rcv.at[slot, values],
-            send_sem=out_sem.at[n],
-            recv_sem=in_sem.at[slot],
-            device_id=device,
-            device_id_type=MESH,
-        )
-        copy.start()
-        sent.append((copy, None))
-
-    def corner_ref(slot):
-        return t2g.at[slot % 2, :, pl.ds(6 if slot < 6 else 0, 2)]
-
-    def send_corner(n):
-        device, slots = to[n]
-        mirrored = first if n < 6 else last
-        source = snd.at[n % 2, :, pl.ds(0 if n < 6 else W - 2, 2)]
-        for slot, chosen in zip(slots, (jnp.logical_not(mirrored), mirrored)):
-            copy = pltpu.make_async_remote_copy(
-                src_ref=source,
-                dst_ref=corner_ref(slot),
-                send_sem=send_sem.at[n],
-                recv_sem=recv_sem.at[slot],
+    early, late = pl.ds(0, EARLY), pl.ds(EARLY, VALUES - EARLY)
+    parts = ((early, send_sem, recv_sem), (late, late_send_sem, late_recv_sem))
+
+    def edge(n, device, slot):
+        return [
+            pltpu.make_async_remote_copy(
+                src_ref=snd.at[n, values],
+                dst_ref=rcv.at[slot, values],
+                send_sem=out_sem.at[n],
+                recv_sem=in_sem.at[slot],
                 device_id=device,
                 device_id_type=MESH,
             )
-            pl.when(jnp.logical_and(chosen, jnp.logical_not(here[n])))(copy.start)
-            if slot == slots[1]:
-                local = pltpu.make_async_copy(source, corner_ref(slot), recv_sem.at[slot])
-                pl.when(jnp.logical_and(chosen, here[n]))(local.start)
-        sent.append((copy, here[n]))
-
-    early, late = pl.ds(0, EARLY), pl.ds(EARLY, VALUES - EARLY)
-    for n in range(2):
-        send_edge(n, early, send_sem, recv_sem)
-    for n in range(4, 8):
-        send_corner(n)
-    for n in range(2, 4):
-        send_edge(n, early, send_sem, recv_sem)
-    for n in range(4):
-        send_edge(n, late, late_send_sem, late_recv_sem)
+            for values, out_sem, in_sem in parts
+        ]
+
+    def corner_ref(side, end):
+        return t2g.at[side, :, pl.ds(0 if end else 6, 2)]
+
+    def send_x(n):
+        for copy in edge(n, *to[n]):
+            copy.start()
+
+    def send_y(side):
+        for copy in edge(side, (gx, jnp.where(side == 0, to[0][0][1], to[1][0][1])), 1 - side):
+            copy.start()
+
+    def send_corners(side):
+        for end in range(2):
+            low, high = to[4 + 2 * end][0], to[5 + 2 * end][0]
+            device = (low[0], jnp.where(side == 0, low[1], high[1]))
+            same = jnp.where(side == 0, here[4 + 2 * end], here[5 + 2 * end])
+            mirrored = (first, last)[end]
+            n = 4 + 2 * end + side
+            source = snd.at[side, :, pl.ds(end * (W - 2), 2)]
+
+            def remote(target, slot):
+                return pltpu.make_async_remote_copy(
+                    src_ref=source,
+                    dst_ref=target,
+                    send_sem=send_sem.at[n],
+                    recv_sem=recv_sem.at[slot],
+                    device_id=device,
+                    device_id_type=MESH,
+                )
+
+            ahead = remote(corner_ref(1 - side, 1 - end), 4 + 2 * (1 - end) + (1 - side))
+            back = remote(corner_ref(side, end), n)
+            local = pltpu.make_async_copy(source, corner_ref(side, end), recv_sem.at[n])
+            pl.when(jnp.logical_not(mirrored))(ahead.start)
+            pl.when(jnp.logical_and(mirrored, jnp.logical_not(same)))(back.start)
+            pl.when(same)(local.start)
+
+    group = lax.rem(gy, 4)
+    odd = lax.rem(lax.div(gx, 2), 2)
+    hasty = jnp.where(group == 0, odd, jnp.where(group == 3, 1, 0))
+    mirrors = ((2, first), (3, last))
+
+    @pl.when(group == 0)
+    def _():
+        for n, mirrored in mirrors:
+            pl.when(jnp.logical_not(mirrored))(lambda: send_x(n))
+
+    send_corners(hasty)
+    send_corners(1 - hasty)
+
+    @pl.when(group == 3)
+    def _():
+        for n, mirrored in mirrors:
+            pl.when(mirrored)(lambda: send_x(n))
+    send_y(hasty)
+
+    @pl.when(group == 2)
+    def _():
+        for n, mirrored in mirrors:
+            pl.when(mirrored)(lambda: send_x(n))
+
+    @pl.when(group != 0)
+    def _():
+        for n, mirrored in mirrors:
+            pl.when(jnp.logical_not(mirrored))(lambda: send_x(n))
+
+    send_y(1 - hasty)
+
+    @pl.when(group < 2)
+    def _():
+        for n, mirrored in mirrors:
+            pl.when(mirrored)(lambda: send_x(n))
 
     def receive(ref, sem):
         pltpu.make_async_copy(ref, ref, sem).wait()
@@ -261,7 +303,7 @@
     end_sign = jnp.where(eight > 5, low_sign, jnp.where(eight < 2, high_sign, 1.0))
 
     def strip(s):
-        ring = s < 2
+        ring = isinstance(s, int)
         n = RING if ring else W
 
         def value(row, index):
@@ -280,7 +322,7 @@
                 for e in range(6):
                     entry = lookup(codes[0:W], e)
                     if e > 3 and not ring:
-                        entry = entry * (low_sign if s == 2 else high_sign)
+                        entry = entry * jnp.where(s == 2, low_sign, high_sign)
                     c_strip[s, row, e, 0:W] = entry
             if ring:
                 for e in range(6):
@@ -303,9 +345,6 @@
             part[row] = [0.0625 * (near[k] + far[k] - v_sum[k]) for k in range(3)]
             inverse[row] = [16.0 / (48.0 * c[row][k] + c_sum[row][k]) for k in range(3)]
 
-        receive(rcv.at[s, late], late_recv_sem.at[s])
-        if not ring:
-            turn_strip(s, range(EARLY, VALUES))
         d = {}
         for row in (1, 2):
             d[row] = []
@@ -325,29 +364,36 @@
         d_sum = [weigh(d[2][k])[0:W] for k in range(3)]
         v_sum = [weigh(v[2][k])[0:W] for k in range(3)]
         near = sym_apply(c3, d_sum)
-        nearer, farther = sides[s % 2]
         if ring:
+            nearer, farther = sides[s]
             rows_0, rows_1 = pl.ds(nearer, W, stride=W), pl.ds(farther, W, stride=W)
         else:
-            rows_0, rows_1 = line(nearer), line(farther)
+            nearer = jnp.where(s == 2, 0, W - 1)
+            rows_0, rows_1 = line(nearer), line(jnp.where(s == 2, 1, W - 2))
         for k in range(3):
             r_own[k, rows_0] = r_own[k, rows_0] - 0.0625 * outer[k]
             r_own[k, rows_1] = r_own[k, rows_1] + 0.0625 * (near[k] + v_sum[k])
             d_own[k, rows_0] = d2[k]
             inv_own[k, rows_0] = inverse[2][k][0:W]
 
-    def turn_strip(s, indices):
-        @pl.when(first if s == 2 else last)
+    def turn_strip(s):
+        @pl.when(jnp.logical_or(first, last))
         def _():
-            for i in indices:
+            for i in range(VALUES):
                 head, tail = rcv[s, i, 0:8], rcv[s, i, 8:W]
                 rcv[s, i, 0:8] = SIGNS[i] * turned(tail)
                 rcv[s, i, 8:W] = SIGNS[i] * turned(head)
 
-    for s in (2, 3):
+    def receive_edge(s):
         receive(rcv.at[s, early], recv_sem.at[s])
-        turn_strip(s, range(EARLY))
-        strip(s)
+        receive(rcv.at[s, late], late_recv_sem.at[s])
+
+    side_a = jnp.where(first, 3, 2)
+    side_b = 5 - side_a
+    receive_edge(side_a)
+    strip(side_a)
+    receive_edge(side_b)
+    turn_strip(side_b)
 
     for s in range(2):
         for j in range(2):
@@ -361,10 +407,10 @@
                     for c in range(3):
                         t2o[s, EARLY + c, spot[0]] = rcv[side, EARLY + c, at]
 
-    for s in (1, 0):
-        receive(rcv.at[s, early], recv_sem.at[s])
-        for slot in (4 + s, 6 + s):
-            receive(corner_ref(slot), recv_sem.at[slot])
+    def receive_y(s):
+        receive_edge(s)
+        for end in range(2):
+            receive(corner_ref(s, end), recv_sem.at[4 + 2 * end + s])
         for mirrored, base in ((first, 6), (last, 0)):
 
             @pl.when(mirrored)
@@ -374,13 +420,21 @@
                     t2g[s, i, base] = SIGNS[i] * two
                     t2g[s, i, base + 1] = SIGNS[i] * one
 
-        strip(s)
-
-    for copy, same in sent:
-        if same is None:
+    receive_y(1)
+    strip(side_b)
+    strip(1)
+    receive_y(0)
+    strip(0)
+
+    for n in range(4):
+        for copy in edge(n, *to[n]):
             copy.wait_send()
-        else:
-            pl.when(jnp.logical_not(same))(copy.wait_send)
+    for n in range(4, 8):
+
+        @pl.when(jnp.logical_not(here[n]))
+        def _():
+            source = snd.at[n % 2, :, pl.ds(0 if n < 6 else W - 2, 2)]
+            pltpu.make_async_copy(source, source, send_sem.at[n]).wait()
 
 
 def finish(u, r, d, inv, out_u, out_r, result, sem):

time: 21.1 us -> 19.4 us (0.919)
  the two profiles are of different devices: /device:TPU:49 before, /device:TPU:89 now
where the time goes in v4:
time: 19.4 us; the launch traced here: 19.3 us
  Pallas kernels  18.7 us (96%)
  between operations  0.64 us (3%)
    pallas_call x1, Pallas kernels, body(): pl.pallas_call(kernel, out_shape=[pltpu.VMEM(field, f32)] * 4, in_specs=[...  17.8 us
    pallas_call x1, Pallas kernels, body(): pl.pallas_call(finish, out_shape=[jax.ShapeDtypeStruct(field, f32)] * 2,...  0.91 us

profile of v4, /device:TPU:89, one launch (start us, length us, event | category | flops | bytes accessed | tf_op | source)
XLA Modules:
  0.0 19.3 jit_solution(6576416107500940173)
XLA Ops:
  0.6 17.8 %shard_map.68 = (f32[3,256,128]{2,1,0:T(8,128)S(1)}, f32[3,256,128]{2,1,0:T(8,128)S(1)}, f32[3,256,128]{2,1,0:T(8,128)S(1)}, f32[3,256,128]{2,1,0:T(8,128)S(1)}) custom-call(f32[3,256,128]{2,1,0:T(8,128)} %bitcast.6, f32[3,256,128]{2,1,0:T(8,128)} %bitcast.7, s32[256,128]{1,0:T(8,128)} %bitcast.8, s32[256,128]{1,0:T(8,128)} %bitcast.9, f32[6,48]{1,0:T(8,128)} %stiffness.1), custom_call_target="tpu_custom_call" | custom-call | tf_op jit(solution)/shard_map/pallas_call | solution.py:470
  18.4 0.9 %shard_map.69 = (f32[3,256,128]{2,1,0:T(8,128)}, f32[3,256,128]{2,1,0:T(8,128)}) custom-call(f32[3,256,128]{2,1,0:T(8,128)S(1)} %get-tuple-element.8.u, f32[3,256,128]{2,1,0:T(8,128)S(1)} %get-tuple-element.9.r, f32[3,256,128]{2,1,0:T(8,128)S(1)} %get-tuple-element.10.d, f32[3,256,128]{2,1,0:T(8,128)S(1)} %get-tuple-element.11.inv), custom_call_target="tpu_custom_call" | custom-call | tf_op jit(solution)/shard_map/pallas_call | solution.py:500

commit v5 on v4

--- a/solution.py
+++ b/solution.py
@@ -19,9 +19,10 @@
 
 W = 16
 RING = W + 8
+CODES, ENDS, PART, LINES = 3 * W, 5 * W, 5 * W + 8, 8 * W + 8
 VALUES = 11
-EARLY = 8
-SIGNS = (-1.0, -1.0, 1.0) * 2 + (1.0, 1.0) + (-1.0, -1.0, 1.0)
+VECTOR = (-1.0, -1.0, 1.0)
+SIGNS = VECTOR * 2 + (1.0, 1.0) + VECTOR
 
 
 def routes(gx, gy):
@@ -66,6 +67,14 @@
     return (h + h) + (below + above)
 
 
+def along_open_row(h):
+    place = lax.broadcasted_iota(jnp.int32, h.shape, 0)
+    n = h.shape[0]
+    below = jnp.where(place == 0, 0.0, pltpu.roll(h, 1, 0))
+    above = jnp.where(place == n - 1, 0.0, pltpu.roll(h, n - 1, 0))
+    return (h + h) + (below + above)
+
+
 def weigh(h, repeat=False):
     return along_depth(along_row(h), repeat)
 
@@ -76,7 +85,7 @@
 
 def kernel(
     load, guess, labels, segments, stiffness, u_own, r_own, d_own, inv_own,
-    blocks, table, l_own, k_own, lab, seg, c_own, v_own, cs_own, snd, rcv, t2g, t2o, c_strip,
+    blocks, table, l_own, k_own, lab, seg, c_own, v_own, cs_own, snd, csnd, rcv, t2g, t2o, c_strip,
     local_sem, send_sem, late_send_sem, recv_sem, late_recv_sem,
 ):
     gx, gy = lax.axis_index("gx"), lax.axis_index("gy")
@@ -114,21 +123,57 @@
     fetch[2].wait()
     fetch[3].wait()
     sides = ((0, 1), (W - 1, W - 2))
+
+    def own_rows(s, j):
+        if isinstance(s, int):
+            return pl.ds(sides[s % 2][j], W, stride=W) if s < 2 else line(sides[s % 2][j])
+        return line(jnp.where(s == 2, sides[0][j], sides[1][j]))
+
     for s in range(4):
+        for c in range(3):
+            snd[s, line(c)] = u_own[c, own_rows(s, 0)]
+            for end in range(2):
+                at = sides[s % 2][1]
+                at = (W * (W - 1) * end + at) if s < 2 else (W * at + (W - 1) * end)
+                snd[s, ENDS + 3 * end + c] = u_own[c, at]
         for j in range(2):
-            at = sides[s % 2][j]
-            rows = pl.ds(at, W, stride=W) if s < 2 else line(at)
-            for c in range(3):
-                snd[s, 3 * j + c] = u_own[c, rows]
-                if j == 0:
-                    snd[s, EARLY + c] = l_own[c, rows]
-            snd[s, 6 + j] = k_own[rows]
+            snd[s, line(3 + j)] = k_own[own_rows(s, j)]
+    for s in range(2):
+        for end in range(2):
+            for j in range(2):
+                at = sides[s][j] + W * (W - 2) * end
+                for i in range(2):
+                    for c in range(3):
+                        csnd[s, end, 3 * j + c, i] = u_own[c, at + W * i]
+                        if j == 0:
+                            csnd[s, end, 8 + c, i] = l_own[c, at + W * i]
+                    csnd[s, end, 6 + j, i] = k_own[at + W * i]
     fetch[4].wait()
     table[0:6, 0 : stiffness.shape[1]] = blocks[...]
 
+    def lookup(codes, entry):
+        rows = jnp.broadcast_to(table[entry : entry + 1, :], codes.shape)
+        return jnp.take_along_axis(rows, codes, axis=1, mode="promise_in_bounds")
+
+    for s in range(4):
+        c, u = [], []
+        for j in range(2):
+            codes = snd[s, line(3 + j)].astype(jnp.int32)
+            c.append([lookup(codes, e) for e in range(6)])
+            u.append([u_own[k, own_rows(s, j)] for k in range(3)])
+            for e in range(6):
+                c_strip[s, 2 + j, e, 0:W] = c[j][e]
+        v = [sym_apply(c[j], u[j]) for j in range(2)]
+        u_sum = [along_depth(along_open_row(2.0 * u[0][k] + u[1][k])) for k in range(3)]
+        v_sum = [along_depth(along_open_row(2.0 * v[0][k] + v[1][k])) for k in range(3)]
+        near = sym_apply(c[0], [64.0 * u[0][k] - u_sum[k] for k in range(3)])
+        for k in range(3):
+            part = l_own[k, own_rows(s, 0)] - 0.0625 * (near[k] - v_sum[k])
+            snd[s, pl.ds(PART + W * k, W)] = part
+
     pl.semaphore_wait(barrier, expected)
 
-    early, late = pl.ds(0, EARLY), pl.ds(EARLY, VALUES - EARLY)
+    early, late = pl.ds(0, PART), pl.ds(PART, LINES - PART)
     parts = ((early, send_sem, recv_sem), (late, late_send_sem, late_recv_sem))
 
     def edge(n, device, slot):
@@ -162,7 +207,7 @@
             same = jnp.where(side == 0, here[4 + 2 * end], here[5 + 2 * end])
             mirrored = (first, last)[end]
             n = 4 + 2 * end + side
-            source = snd.at[side, :, pl.ds(end * (W - 2), 2)]
+            source = csnd.at[side, end]
 
             def remote(target, slot):
                 return pltpu.make_async_remote_copy(
@@ -220,10 +265,6 @@
     def receive(ref, sem):
         pltpu.make_async_copy(ref, ref, sem).wait()
 
-    def lookup(codes, entry):
-        rows = jnp.broadcast_to(table[entry : entry + 1, :], codes.shape)
-        return jnp.take_along_axis(rows, codes, axis=1, mode="promise_in_bounds")
-
     inner_row = lax.broadcasted_iota(jnp.int32, (W, 128), 0)
     inner_row = jnp.logical_and(inner_row > 0, inner_row < W - 1)
     none = jnp.zeros((W, 128), f32)
@@ -242,12 +283,6 @@
         v = sym_apply(c, [u_own[k, line(x)] for k in range(3)])
         for k in range(3):
             v_own[k, line(x)] = v[k]
-
-    for s in range(4):
-        for j in range(2):
-            codes = snd[s, 6 + j].astype(jnp.int32)
-            for e in range(6):
-                c_strip[s, 2 + j, e, 0:W] = lookup(codes, e)
 
     def three(ref, e, x):
         return (ref[e, line(x - 1)] + ref[e, line(x + 1)]) + 2.0 * ref[e, line(x)]
@@ -306,50 +341,79 @@
         ring = isinstance(s, int)
         n = RING if ring else W
 
-        def value(row, index):
-            own = row > 1
-            if not ring:
-                return (snd if own else rcv)[s, index]
-            ends = t2o if own else t2g
-            return jnp.concatenate([(snd if own else rcv)[s, index], ends[s, index]], axis=0)
-
-        def layer(row):
-            return (1, 0, 0, 1)[row]
-
+        def ringed(row, index, middle):
+            return jnp.concatenate([middle, (t2g if row < 2 else t2o)[s, index]], axis=0)
+
+        place = lax.broadcasted_iota(jnp.int32, (W, 128), 0)
+        c, u = [], []
         for row in range(4):
-            codes = value(row, 6 + layer(row)).astype(jnp.int32)
+            layer = (1, 0, 0, 1)[row]
+            codes = (rcv if row < 2 else snd)[s, line(3 + layer)].astype(jnp.int32)
             if row < 2:
                 for e in range(6):
-                    entry = lookup(codes[0:W], e)
+                    entry = lookup(codes, e)
                     if e > 3 and not ring:
                         entry = entry * jnp.where(s == 2, low_sign, high_sign)
                     c_strip[s, row, e, 0:W] = entry
             if ring:
+                codes = (t2g if row < 2 else t2o)[s, 6 + layer].astype(jnp.int32)
                 for e in range(6):
-                    entry = lookup(codes[W:RING], e)
+                    entry = lookup(codes, e)
                     c_strip[s, row, e, W:RING] = entry * end_sign if e > 3 else entry
-        c = [[c_strip[s, row, e, 0:n] for e in range(6)] for row in range(4)]
-        u = [[value(row, 3 * layer(row) + k) for k in range(3)] for row in range(4)]
-        v = [sym_apply(c[row], u[row]) for row in range(4)]
+            c.append([c_strip[s, row, e, 0:n] for e in range(6)])
+            u.append([])
+            for k in range(3):
+                if row == 0:
+                    low_end = jnp.broadcast_to(rcv[s, pl.ds(ENDS + k, 1)], (W, 128))
+                    high_end = jnp.broadcast_to(rcv[s, pl.ds(ENDS + 3 + k, 1)], (W, 128))
+                    middle = jnp.where(place == 0, low_end, 0.0)
+                    middle = jnp.where(place == W - 1, high_end, middle)
+                elif row == 1:
+                    middle = rcv[s, line(k)]
+                else:
+                    middle = u_own[k, own_rows(s, layer)]
+                u[row].append(ringed(row, 3 * layer + k, middle) if ring else middle)
+        v = [sym_apply(c[row], u[row]) if ring or row > 0 else None for row in range(4)]
 
         def three_rows(f, row, k):
             return (f[row - 1][k] + f[row + 1][k]) + 2.0 * f[row][k]
 
+        def sums(f, row, k):
+            if not ring:
+                return weigh(f[2][k] if row == 1 else three_rows(f, row, k))
+            whole = three_rows(f, row, k)
+            rest = jnp.concatenate(
+                [f[2][k][0:W], whole[W:RING]] if row == 1 else [whole[0:W], f[1][k][W:RING]],
+                axis=0,
+            )
+            middle, ends = (rest, whole) if row == 1 else (whole, rest)
+            h = jnp.concatenate([along_row(middle)[0:W], along_row(ends)[W:RING]], axis=0)
+            return along_depth(h)
+
+        tail = (lax.broadcasted_iota(jnp.int32, (n, 128), 0) >= W) if ring else None
+        raw = {1: jnp.where(tail, 64.0, 0.0) if ring else 0.0, 2: jnp.where(tail, 0.0, 64.0) if ring else 64.0}
         part, inverse, c_sum = {}, {}, {}
         for row in (1, 2):
             c_sum[row] = [weigh(three_rows(c, row, e), True) for e in range(6)]
-            u_sum = [weigh(three_rows(u, row, k)) for k in range(3)]
-            v_sum = [weigh(three_rows(v, row, k)) for k in range(3)]
-            near = sym_apply(c[row], [64.0 * u[row][k] - u_sum[k] for k in range(3)])
+            u_sum = [sums(u, row, k) for k in range(3)]
+            v_sum = [sums(v, row, k) for k in range(3)]
+            near = sym_apply(c[row], [raw[row] * u[row][k] - u_sum[k] for k in range(3)])
             far = sym_apply(c_sum[row], u[row])
             part[row] = [0.0625 * (near[k] + far[k] - v_sum[k]) for k in range(3)]
             inverse[row] = [16.0 / (48.0 * c[row][k] + c_sum[row][k]) for k in range(3)]
+
+        def start_of(row, k):
+            if row == 1:
+                middle = rcv[s, pl.ds(PART + W * k, W)]
+            else:
+                middle = l_own[k, own_rows(s, 0)]
+            return ringed(row, 8 + k, middle) if ring else middle
 
         d = {}
         for row in (1, 2):
             d[row] = []
             for k in range(3):
-                r = value(row, EARLY + k) - part[row][k]
+                r = start_of(row, k) - part[row][k]
                 step = u[row][k] + (inverse[row][k] * r) * (1.0 / theta_value)
                 d[row].append(step if ring else jnp.where(inner_row, step, 0.0))
         v = {row: sym_apply(c[row], d[row]) for row in (1, 2)}
@@ -379,10 +443,15 @@
     def turn_strip(s):
         @pl.when(jnp.logical_or(first, last))
         def _():
-            for i in range(VALUES):
-                head, tail = rcv[s, i, 0:8], rcv[s, i, 8:W]
-                rcv[s, i, 0:8] = SIGNS[i] * turned(tail)
-                rcv[s, i, 8:W] = SIGNS[i] * turned(head)
+            lines = [W * i for i in range(5)] + [PART + W * k for k in range(3)]
+            for at, sign in zip(lines, VECTOR + (1.0, 1.0) + VECTOR):
+                head, tail = rcv[s, at : at + 8], rcv[s, at + 8 : at + W]
+                rcv[s, at : at + 8] = sign * turned(tail)
+                rcv[s, at + 8 : at + W] = sign * turned(head)
+            for k in range(3):
+                one, two = rcv[s, ENDS + k], rcv[s, ENDS + 3 + k]
+                rcv[s, ENDS + k] = VECTOR[k] * two
+                rcv[s, ENDS + 3 + k] = VECTOR[k] * one
 
     def receive_edge(s):
         receive(rcv.at[s, early], recv_sem.at[s])
@@ -399,13 +468,13 @@
         for j in range(2):
             at = sides[s][j]
             for side, spot in ((2, (7, 6)), (3, (0, 1))):
+                for c in range(3):
+                    t2o[s, 3 * j + c, spot[0]] = rcv[side, W * c + at]
+                    if j == 0:
+                        t2o[s, c, spot[1]] = rcv[side, ENDS + 3 * s + c]
+                        t2o[s, 8 + c, spot[0]] = rcv[side, PART + W * c + at]
                 for i in range(2):
-                    for c in range(3):
-                        t2o[s, 3 * j + c, spot[i]] = rcv[side, 3 * i + c, at]
-                    t2o[s, 6 + j, spot[i]] = rcv[side, 6 + i, at]
-                if j == 0:
-                    for c in range(3):
-                        t2o[s, EARLY + c, spot[0]] = rcv[side, EARLY + c, at]
+                    t2o[s, 6 + j, spot[i]] = rcv[side, CODES + W * i + at]
 
     def receive_y(s):
         receive_edge(s)
@@ -433,7 +502,7 @@
 
         @pl.when(jnp.logical_not(here[n]))
         def _():
-            source = snd.at[n % 2, :, pl.ds(0 if n < 6 else W - 2, 2)]
+            source = csnd.at[n % 2, n // 6]
             pltpu.make_async_copy(source, source, send_sem.at[n]).wait()
 
 
@@ -482,8 +551,9 @@
             pltpu.VMEM((6,) + field[1:], f32),
             pltpu.VMEM(field, f32),
             pltpu.VMEM((6,) + field[1:], f32),
-            pltpu.VMEM((4, VALUES, W, 128), f32),
-            pltpu.VMEM((4, VALUES, W, 128), f32),
+            pltpu.VMEM((4, LINES, 128), f32),
+            pltpu.VMEM((2, 2, VALUES, 2, 128), f32),
+            pltpu.VMEM((4, LINES, 128), f32),
             pltpu.VMEM((2, VALUES, 8, 128), f32),
             pltpu.VMEM((2, VALUES, 8, 128), f32),
             pltpu.VMEM((4, 4, 6, RING, 128), f32),

time: 19.4 us -> 18.4 us (0.948)
  the two profiles are of different devices: /device:TPU:89 before, /device:TPU:8 now
where the time goes in v5:
time: 18.4 us; the launch traced here: 18.3 us
  Pallas kernels  17.6 us (96%)
  between operations  0.64 us (3%)
    pallas_call x1, Pallas kernels, body(): pl.pallas_call(kernel, out_shape=[pltpu.VMEM(field, f32)] * 4, in_specs=[...  16.7 us
    pallas_call x1, Pallas kernels, body(): pl.pallas_call(finish, out_shape=[jax.ShapeDtypeStruct(field, f32)] * 2,...  0.91 us

profile of v5, /device:TPU:8, one launch (start us, length us, event | category | flops | bytes accessed | tf_op | source)
XLA Modules:
  0.0 18.3 jit_solution(6650808846036491138)
XLA Ops:
  0.6 16.7 %shard_map.68 = (f32[3,256,128]{2,1,0:T(8,128)S(1)}, f32[3,256,128]{2,1,0:T(8,128)S(1)}, f32[3,256,128]{2,1,0:T(8,128)S(1)}, f32[3,256,128]{2,1,0:T(8,128)S(1)}) custom-call(f32[3,256,128]{2,1,0:T(8,128)} %bitcast.6, f32[3,256,128]{2,1,0:T(8,128)} %bitcast.7, s32[256,128]{1,0:T(8,128)} %bitcast.8, s32[256,128]{1,0:T(8,128)} %bitcast.9, f32[6,48]{1,0:T(8,128)} %stiffness.1), custom_call_target="tpu_custom_call" | custom-call | tf_op jit(solution)/shard_map/pallas_call | solution.py:539
  17.4 0.9 %shard_map.69 = (f32[3,256,128]{2,1,0:T(8,128)}, f32[3,256,128]{2,1,0:T(8,128)}) custom-call(f32[3,256,128]{2,1,0:T(8,128)S(1)} %get-tuple-element.8.u, f32[3,256,128]{2,1,0:T(8,128)S(1)} %get-tuple-element.9.r, f32[3,256,128]{2,1,0:T(8,128)S(1)} %get-tuple-element.10.d, f32[3,256,128]{2,1,0:T(8,128)S(1)} %get-tuple-element.11.inv), custom_call_target="tpu_custom_call" | custom-call | tf_op jit(solution)/shard_map/pallas_call | solution.py:570

commit v6 on v5

--- a/solution.py
+++ b/solution.py
@@ -93,9 +93,9 @@
     fetch = [
         pltpu.make_async_copy(labels, lab, local_sem.at[0]),
         pltpu.make_async_copy(segments, seg, local_sem.at[1]),
+        pltpu.make_async_copy(stiffness, blocks, local_sem.at[4]),
         pltpu.make_async_copy(guess, u_own, local_sem.at[2]),
         pltpu.make_async_copy(load, l_own, local_sem.at[3]),
-        pltpu.make_async_copy(stiffness, blocks, local_sem.at[4]),
     ]
     for copy in fetch:
         copy.start()
@@ -120,8 +120,8 @@
     fetch[0].wait()
     fetch[1].wait()
     k_own[...] = (lab[...] * SEGS + seg[...]).astype(f32)
-    fetch[2].wait()
     fetch[3].wait()
+    fetch[4].wait()
     sides = ((0, 1), (W - 1, W - 2))
 
     def own_rows(s, j):
@@ -148,7 +148,7 @@
                         if j == 0:
                             csnd[s, end, 8 + c, i] = l_own[c, at + W * i]
                     csnd[s, end, 6 + j, i] = k_own[at + W * i]
-    fetch[4].wait()
+    fetch[2].wait()
     table[0:6, 0 : stiffness.shape[1]] = blocks[...]
 
     def lookup(codes, entry):
@@ -409,6 +409,8 @@
                 middle = l_own[k, own_rows(s, 0)]
             return ringed(row, 8 + k, middle) if ring else middle
 
+        if ring:
+            receive(rcv.at[s, late], late_recv_sem.at[s])
         d = {}
         for row in (1, 2):
             d[row] = []
@@ -477,7 +479,7 @@
                     t2o[s, 6 + j, spot[i]] = rcv[side, CODES + W * i + at]
 
     def receive_y(s):
-        receive_edge(s)
+        receive(rcv.at[s, early], recv_sem.at[s])
         for end in range(2):
             receive(corner_ref(s, end), recv_sem.at[4 + 2 * end + s])
         for mirrored, base in ((first, 6), (last, 0)):

time: 18.4 us -> 18.1 us (0.984)
  the two profiles are of different devices: /device:TPU:8 before, /device:TPU:49 now
where the time goes in v6:
time: 18.1 us; the launch traced here: 17.9 us
  Pallas kernels  17.3 us (96%)
  between operations  0.64 us (4%)
    pallas_call x1, Pallas kernels, body(): pl.pallas_call(kernel, out_shape=[pltpu.VMEM(field, f32)] * 4, in_specs=[...  16.4 us
    pallas_call x1, Pallas kernels, body(): pl.pallas_call(finish, out_shape=[jax.ShapeDtypeStruct(field, f32)] * 2,...  0.91 us

profile of v6, /device:TPU:49, one launch (start us, length us, event | category | flops | bytes accessed | tf_op | source)
XLA Modules:
  0.0 17.9 jit_solution(4296977224637618485)
XLA Ops:
  0.6 16.4 %shard_map.68 = (f32[3,256,128]{2,1,0:T(8,128)S(1)}, f32[3,256,128]{2,1,0:T(8,128)S(1)}, f32[3,256,128]{2,1,0:T(8,128)S(1)}, f32[3,256,128]{2,1,0:T(8,128)S(1)}) custom-call(f32[3,256,128]{2,1,0:T(8,128)} %bitcast.6, f32[3,256,128]{2,1,0:T(8,128)} %bitcast.7, s32[256,128]{1,0:T(8,128)} %bitcast.8, s32[256,128]{1,0:T(8,128)} %bitcast.9, f32[6,48]{1,0:T(8,128)} %stiffness.1), custom_call_target="tpu_custom_call" | custom-call | tf_op jit(solution)/shard_map/pallas_call | solution.py:541
  17.0 0.9 %shard_map.69 = (f32[3,256,128]{2,1,0:T(8,128)}, f32[3,256,128]{2,1,0:T(8,128)}) custom-call(f32[3,256,128]{2,1,0:T(8,128)S(1)} %get-tuple-element.8.u, f32[3,256,128]{2,1,0:T(8,128)S(1)} %get-tuple-element.9.r, f32[3,256,128]{2,1,0:T(8,128)S(1)} %get-tuple-element.10.d, f32[3,256,128]{2,1,0:T(8,128)S(1)} %get-tuple-element.11.inv), custom_call_target="tpu_custom_call" | custom-call | tf_op jit(solution)/shard_map/pallas_call | solution.py:572

commit v7 on v6

--- a/solution.py
+++ b/solution.py
@@ -176,6 +176,11 @@
     early, late = pl.ds(0, PART), pl.ds(PART, LINES - PART)
     parts = ((early, send_sem, recv_sem), (late, late_send_sem, late_recv_sem))
 
+    whole = ((pl.ds(0, LINES), send_sem, recv_sem),)
+
+    def n_is_y(n):
+        return not isinstance(n, int) or n < 2
+
     def edge(n, device, slot):
         return [
             pltpu.make_async_remote_copy(
@@ -186,7 +191,7 @@
                 device_id=device,
                 device_id_type=MESH,
             )
-            for values, out_sem, in_sem in parts
+            for values, out_sem, in_sem in (parts if n_is_y(n) else whole)
         ]
 
     def corner_ref(side, end):
@@ -233,8 +238,10 @@
 
     @pl.when(group == 0)
     def _():
-        for n, mirrored in mirrors:
-            pl.when(jnp.logical_not(mirrored))(lambda: send_x(n))
+        upper = lax.rem(gx, 2) == 1
+        pl.when(jnp.logical_and(upper, jnp.logical_not(last)))(lambda: send_x(3))
+        pl.when(jnp.logical_not(first))(lambda: send_x(2))
+        pl.when(jnp.logical_not(jnp.logical_or(upper, last)))(lambda: send_x(3))
 
     send_corners(hasty)
     send_corners(1 - hasty)
@@ -456,10 +463,9 @@
                 rcv[s, ENDS + 3 + k] = VECTOR[k] * one
 
     def receive_edge(s):
-        receive(rcv.at[s, early], recv_sem.at[s])
-        receive(rcv.at[s, late], late_recv_sem.at[s])
-
-    side_a = jnp.where(first, 3, 2)
+        receive(rcv.at[s], recv_sem.at[s])
+
+    side_a = jnp.where(lax.rem(gx, 2) == 0, 3, 2)
     side_b = 5 - side_a
     receive_edge(side_a)
     strip(side_a)

time: 18.1 us -> 18.1 us (level)
  no operation moved by 1% of the time
where the time goes in v7:
time: 18.1 us; the launch traced here: 17.9 us
  Pallas kernels  17.3 us (96%)
  between operations  0.64 us (4%)
    pallas_call x1, Pallas kernels, body(): pl.pallas_call(kernel, out_shape=[pltpu.VMEM(field, f32)] * 4, in_specs=[...  16.4 us
    pallas_call x1, Pallas kernels, body(): pl.pallas_call(finish, out_shape=[jax.ShapeDtypeStruct(field, f32)] * 2,...  0.91 us

profile of v7, /device:TPU:49, one launch (start us, length us, event | category | flops | bytes accessed | tf_op | source)
XLA Modules:
  0.0 17.9 jit_solution(18179854440988304979)
XLA Ops:
  0.6 16.4 %shard_map.68 = (f32[3,256,128]{2,1,0:T(8,128)S(1)}, f32[3,256,128]{2,1,0:T(8,128)S(1)}, f32[3,256,128]{2,1,0:T(8,128)S(1)}, f32[3,256,128]{2,1,0:T(8,128)S(1)}) custom-call(f32[3,256,128]{2,1,0:T(8,128)} %bitcast.6, f32[3,256,128]{2,1,0:T(8,128)} %bitcast.7, s32[256,128]{1,0:T(8,128)} %bitcast.8, s32[256,128]{1,0:T(8,128)} %bitcast.9, f32[6,48]{1,0:T(8,128)} %stiffness.1), custom_call_target="tpu_custom_call" | custom-call | tf_op jit(solution)/shard_map/pallas_call | solution.py:547
  17.0 0.9 %shard_map.69 = (f32[3,256,128]{2,1,0:T(8,128)}, f32[3,256,128]{2,1,0:T(8,128)}) custom-call(f32[3,256,128]{2,1,0:T(8,128)S(1)} %get-tuple-element.8.u, f32[3,256,128]{2,1,0:T(8,128)S(1)} %get-tuple-element.9.r, f32[3,256,128]{2,1,0:T(8,128)S(1)} %get-tuple-element.10.d, f32[3,256,128]{2,1,0:T(8,128)S(1)} %get-tuple-element.11.inv), custom_call_target="tpu_custom_call" | custom-call | tf_op jit(solution)/shard_map/pallas_call | solution.py:578

commit v8 on v7

--- a/solution.py
+++ b/solution.py
@@ -19,6 +19,8 @@
 
 W = 16
 RING = W + 8
+CELLS = W * W
+ROOM = CELLS + W
 CODES, ENDS, PART, LINES = 3 * W, 5 * W, 5 * W + 8, 8 * W + 8
 VALUES = 11
 VECTOR = (-1.0, -1.0, 1.0)
@@ -94,8 +96,8 @@
         pltpu.make_async_copy(labels, lab, local_sem.at[0]),
         pltpu.make_async_copy(segments, seg, local_sem.at[1]),
         pltpu.make_async_copy(stiffness, blocks, local_sem.at[4]),
-        pltpu.make_async_copy(guess, u_own, local_sem.at[2]),
-        pltpu.make_async_copy(load, l_own, local_sem.at[3]),
+        pltpu.make_async_copy(guess, u_own.at[:, pl.ds(0, CELLS)], local_sem.at[2]),
+        pltpu.make_async_copy(load, l_own.at[:, pl.ds(0, CELLS)], local_sem.at[3]),
     ]
     for copy in fetch:
         copy.start()
@@ -119,7 +121,7 @@
     t2o[...] = jnp.zeros(t2o.shape, f32)
     fetch[0].wait()
     fetch[1].wait()
-    k_own[...] = (lab[...] * SEGS + seg[...]).astype(f32)
+    k_own[0:CELLS] = (lab[...] * SEGS + seg[...]).astype(f32)
     fetch[3].wait()
     fetch[4].wait()
     sides = ((0, 1), (W - 1, W - 2))
@@ -515,7 +517,7 @@
 
 
 def finish(u, r, d, inv, out_u, out_r, result, sem):
-    copies = [pltpu.make_async_copy(r, out_r, sem.at[3])]
+    copies = [pltpu.make_async_copy(r.at[:, pl.ds(0, CELLS)], out_r, sem.at[3])]
     copies[0].start()
     for k in range(3):
         copies.append(pltpu.make_async_copy(result.at[k], out_u.at[k], sem.at[k]))
@@ -546,14 +548,14 @@
     )
     results = pl.pallas_call(
         kernel,
-        out_shape=[pltpu.VMEM(field, f32)] * 4,
+        out_shape=[pltpu.VMEM((3, ROOM, 128), f32)] * 4,
         in_specs=[hbm] * 5,
         out_specs=[vmem] * 4,
         scratch_shapes=[
             pltpu.VMEM(stiffness.shape, f32),
             pltpu.VMEM((8, 128), f32),
-            pltpu.VMEM(field, f32),
-            pltpu.VMEM(field[1:], f32),
+            pltpu.VMEM((3, ROOM, 128), f32),
+            pltpu.VMEM((ROOM, 128), f32),
             pltpu.VMEM(field[1:], jnp.int32),
             pltpu.VMEM(field[1:], jnp.int32),
             pltpu.VMEM((6,) + field[1:], f32),

time: 18.1 us -> 18.1 us (level)
  no operation moved by 1% of the time
where the time goes in v8:
time: 18.1 us; the launch traced here: 17.9 us
  Pallas kernels  17.3 us (96%)
  between operations  0.64 us (4%)
    pallas_call x1, Pallas kernels, body(): pl.pallas_call(kernel, out_shape=[pltpu.VMEM((3, ROOM, 128), f32)] * 4, i...  16.4 us
    pallas_call x1, Pallas kernels, body(): pl.pallas_call(finish, out_shape=[jax.ShapeDtypeStruct(field, f32)] * 2,...  0.91 us

profile of v8, /device:TPU:49, one launch (start us, length us, event | category | flops | bytes accessed | tf_op | source)
XLA Modules:
  0.0 17.9 jit_solution(2052381987807320227)
XLA Ops:
  0.6 16.4 %shard_map.68 = (f32[3,272,128]{2,1,0:T(8,128)S(1)}, f32[3,272,128]{2,1,0:T(8,128)S(1)}, f32[3,272,128]{2,1,0:T(8,128)S(1)}, f32[3,272,128]{2,1,0:T(8,128)S(1)}) custom-call(f32[3,256,128]{2,1,0:T(8,128)} %bitcast.6, f32[3,256,128]{2,1,0:T(8,128)} %bitcast.7, s32[256,128]{1,0:T(8,128)} %bitcast.8, s32[256,128]{1,0:T(8,128)} %bitcast.9, f32[6,48]{1,0:T(8,128)} %stiffness.1), custom_call_target="tpu_custom_call" | custom-call | tf_op jit(solution)/shard_map/pallas_call | solution.py:549
  17.0 0.9 %shard_map.69 = (f32[3,256,128]{2,1,0:T(8,128)}, f32[3,256,128]{2,1,0:T(8,128)}) custom-call(f32[3,272,128]{2,1,0:T(8,128)S(1)} %get-tuple-element.8.u, f32[3,272,128]{2,1,0:T(8,128)S(1)} %get-tuple-element.9.r, f32[3,272,128]{2,1,0:T(8,128)S(1)} %get-tuple-element.10.d, f32[3,272,128]{2,1,0:T(8,128)S(1)} %get-tuple-element.11.inv), custom_call_target="tpu_custom_call" | custom-call | tf_op jit(solution)/shard_map/pallas_call | solution.py:580

commit v9 on v8

--- a/solution.py
+++ b/solution.py
@@ -92,6 +92,23 @@
 ):
     gx, gy = lax.axis_index("gx"), lax.axis_index("gy")
     first, last = gx == 0, gx == lax.axis_size("gx") - 1
+    t2g[...] = jnp.zeros(t2g.shape, f32)
+
+    to = routes(gx, gy)
+    here = [None] * 4 + [jnp.logical_and(d[0] == gx, d[1] == gy) for d, _ in to[4:]]
+    barrier = pltpu.get_barrier_semaphore()
+    expected = 4
+    for (device, _), same in zip(to, here):
+        if same is None:
+            pl.semaphore_signal(barrier, inc=1, device_id=device, device_id_type=MESH)
+        else:
+
+            @pl.when(jnp.logical_not(same))
+            def _():
+                pl.semaphore_signal(barrier, inc=1, device_id=device, device_id_type=MESH)
+
+            expected = expected + jnp.where(same, 0, 1)
+
     fetch = [
         pltpu.make_async_copy(labels, lab, local_sem.at[0]),
         pltpu.make_async_copy(segments, seg, local_sem.at[1]),
@@ -101,23 +118,6 @@
     ]
     for copy in fetch:
         copy.start()
-    t2g[...] = jnp.zeros(t2g.shape, f32)
-
-    to = routes(gx, gy)
-    here = [None] * 4 + [jnp.logical_and(d[0] == gx, d[1] == gy) for d, _ in to[4:]]
-    barrier = pltpu.get_barrier_semaphore()
-    expected = 4
-    for (device, _), same in zip(to, here):
-        if same is None:
-            pl.semaphore_signal(barrier, inc=1, device_id=device, device_id_type=MESH)
-        else:
-
-            @pl.when(jnp.logical_not(same))
-            def _():
-                pl.semaphore_signal(barrier, inc=1, device_id=device, device_id_type=MESH)
-
-            expected = expected + jnp.where(same, 0, 1)
-
     t2o[...] = jnp.zeros(t2o.shape, f32)
     fetch[0].wait()
     fetch[1].wait()

time: 18.1 us -> 18.2 us (level)
  no operation moved by 1% of the time
where the time goes in v9:
time: 18.2 us; the launch traced here: 17.9 us
  Pallas kernels  17.3 us (95%)
  between operations  0.64 us (4%)
    pallas_call x1, Pallas kernels, body(): pl.pallas_call(kernel, out_shape=[pltpu.VMEM((3, ROOM, 128), f32)] * 4, i...  16.4 us
    pallas_call x1, Pallas kernels, body(): pl.pallas_call(finish, out_shape=[jax.ShapeDtypeStruct(field, f32)] * 2,...  0.91 us

profile of v9, /device:TPU:49, one launch (start us, length us, event | category | flops | bytes accessed | tf_op | source)
XLA Modules:
  0.0 17.9 jit_solution(1059038410696352185)
XLA Ops:
  0.6 16.4 %shard_map.68 = (f32[3,272,128]{2,1,0:T(8,128)S(1)}, f32[3,272,128]{2,1,0:T(8,128)S(1)}, f32[3,272,128]{2,1,0:T(8,128)S(1)}, f32[3,272,128]{2,1,0:T(8,128)S(1)}) custom-call(f32[3,256,128]{2,1,0:T(8,128)} %bitcast.6, f32[3,256,128]{2,1,0:T(8,128)} %bitcast.7, s32[256,128]{1,0:T(8,128)} %bitcast.8, s32[256,128]{1,0:T(8,128)} %bitcast.9, f32[6,48]{1,0:T(8,128)} %stiffness.1), custom_call_target="tpu_custom_call" | custom-call | tf_op jit(solution)/shard_map/pallas_call | solution.py:549
  17.0 0.9 %shard_map.69 = (f32[3,256,128]{2,1,0:T(8,128)}, f32[3,256,128]{2,1,0:T(8,128)}) custom-call(f32[3,272,128]{2,1,0:T(8,128)S(1)} %get-tuple-element.8.u, f32[3,272,128]{2,1,0:T(8,128)S(1)} %get-tuple-element.9.r, f32[3,272,128]{2,1,0:T(8,128)S(1)} %get-tuple-element.10.d, f32[3,272,128]{2,1,0:T(8,128)S(1)} %get-tuple-element.11.inv), custom_call_target="tpu_custom_call" | custom-call | tf_op jit(solution)/shard_map/pallas_call | solution.py:580
